TPU v7x, 256 devices: a whole 4x4x8 slice. The times are simulated.
256 devices in a mesh: gx: 16 (over x, y), gy: 4 (over z_lo, core), gz: 4 (over z_hi).
Axes of the slice: x: 4, y: 4, z: 8 (z_hi: 4, z_lo: 2; z = z_hi * 2 + z_lo), core: 2. Of those that a mesh axis runs over, the one named last changes fastest.
Arguments:
- iterate: float32 [4194304], P(('gx', 'gy', 'gz')), may hold values from -6 to 6
- residual: float32 [4194304], P(('gx', 'gy', 'gz'))
- direction: float32 [4194304], P(('gx', 'gy', 'gz'))
- noise: float32 [4194304], P(('gx', 'gy', 'gz')), may hold values from 0.1 to 1
- stencil_base: int32 [3, 32768], P(None, ('gx', 'gy', 'gz')), may hold values from 0 to 508, as said below
- interp_weights: float32 [12, 4194304], P(None, ('gx', 'gy', 'gz')), may hold values from -0.25 to 1
- tile_counts: int32 [32768], P(('gx', 'gy', 'gz')), may hold values from 42 to 128, as said below
- reach: float32 [3], replicated, may hold values from 1.5 to 6
Outputs:
- new_iterate: float32 [4194304], P(('gx', 'gy', 'gz'))
- new_residual: float32 [4194304], P(('gx', 'gy', 'gz'))
- new_direction: float32 [4194304], P(('gx', 'gy', 'gz'))
Inputs may be any that keep to these rules, and one draw needn't show every extreme that they name: Along each dimension the four stencil cells lie inside the grid, and stencil_base + 1 lies in the block of 32 x 64 x 128 cells of the device that holds the tile (devices taken in the order of the tiles' shards, blocks in the grid's order). `tile_counts`: every device has a tile with all 128 slots live.
All inputs are finite; a program needn't handle non-finite values.
Results may differ from a plain program's by a relative error of at most 0.000059.
Values sent between devices are 32-bit elements; how exact they have to be, the bound alone decides.
A program may use at most 192 MiB of HBM per device.

v0:
```python
import jax
import jax.numpy as jnp
from jax import lax
from jax.sharding import PartitionSpec as P

NX = 512
NY = 256
NZ = 512
SLOT = 128


HIGHEST = lax.Precision.HIGHEST


def with_halo(cells, sides, width):
    for axis, dim in sides:
        count = lax.axis_size(axis)
        ends = count - 1
        head = lax.slice_in_dim(cells, 0, width, axis=dim)
        tail = lax.slice_in_dim(cells, cells.shape[dim] - width, cells.shape[dim], axis=dim)
        cells = jnp.concatenate(
            [
                lax.ppermute(tail, axis, [(i, (i + 1) % count) for i in range(ends)]),
                cells,
                lax.ppermute(head, axis, [((i + 1) % count, i) for i in range(ends)]),
            ],
            axis=dim,
        )
    return cells


def factor_block(row_pos, col_pos, length):
    distance = jnp.abs(row_pos[:, None] - col_pos[None, :])
    return jnp.exp(-distance / length) / jnp.sqrt(length)


def tap_weights(interp_weights):
    along_x = interp_weights[0:4]
    along_y = interp_weights[4:8]
    along_z = interp_weights[8:12]
    product = along_x[:, None, None, :] * along_y[None, :, None, :] * along_z[None, None, :, :]
    return product.reshape(64, -1)


def tap_index(first_x, first_y, first_z, stride_x, stride_y, stride_z):
    offsets = jnp.arange(4, dtype=jnp.int32)[:, None]
    cells_x = (first_x[None, :] + offsets) * stride_x
    cells_y = (first_y[None, :] + offsets) * stride_y
    cells_z = (first_z[None, :] + offsets) * stride_z
    index = cells_x[:, None, None, :] + cells_y[None, :, None, :] + cells_z[None, None, :, :]
    return index.reshape(64, -1)


def body(iterate, residual, direction, noise, stencil_base, interp_weights, tile_counts, reach):
    size_x = NX // lax.axis_size("gx")
    size_y = NY // lax.axis_size("gy")
    size_z = NZ // lax.axis_size("gz")
    wide_x = size_x + 3
    wide_y = size_y + 3
    wide_z = size_z + 3
    index_x = lax.axis_index("gx")
    index_y = lax.axis_index("gy")
    index_z = lax.axis_index("gz")
    anchor_x = index_x * size_x
    anchor_y = index_y * size_y
    anchor_z = index_z * size_z
    length_x = reach[0] * size_x
    length_y = reach[1] * size_y
    length_z = reach[2] * size_z
    own_x = (anchor_x + jnp.arange(size_x, dtype=jnp.int32)).astype(jnp.float32)
    own_y = (anchor_y + jnp.arange(size_y, dtype=jnp.int32)).astype(jnp.float32)
    own_z = (anchor_z + jnp.arange(size_z, dtype=jnp.int32)).astype(jnp.float32)
    tile_total = tile_counts.shape[0]
    slot_place = jnp.arange(SLOT, dtype=jnp.int32)
    live_mask = (slot_place[None, :] < tile_counts[:, None]).reshape(-1).astype(jnp.float32)
    live_dir = live_mask * direction
    live_res = live_mask * residual
    stencil_weights = tap_weights(interp_weights).reshape(64, tile_total, SLOT)
    tile_taps = jnp.sum(stencil_weights * live_dir.reshape(1, tile_total, SLOT), axis=2)
    spread_index = tap_index(
        stencil_base[0] - anchor_x + 1,
        stencil_base[1] - anchor_y + 1,
        stencil_base[2] - anchor_z + 1,
        wide_y * wide_z,
        wide_z,
        1,
    )
    spread_grid = jnp.zeros((wide_x * wide_y * wide_z,), jnp.float32)
    spread_grid = spread_grid.at[spread_index.reshape(-1)].add(tile_taps.reshape(-1))
    spread_grid = spread_grid.reshape(wide_x, wide_y, wide_z)
    piece = lax.all_gather(spread_grid, "gx", axis=0, tiled=True)
    place = jnp.arange(piece.shape[0], dtype=jnp.int32)
    col_pos = (place // wide_x * size_x + place % wide_x - 1).astype(jnp.float32)
    block = factor_block(own_x, col_pos, length_x)
    section_x = jnp.einsum("ij,jkl->ikl", block, piece, precision=HIGHEST)
    piece = lax.all_gather(section_x, "gy", axis=1, tiled=True)
    place = jnp.arange(piece.shape[1], dtype=jnp.int32)
    col_pos = (place // wide_y * size_y + place % wide_y - 1).astype(jnp.float32)
    block = factor_block(own_y, col_pos, length_y)
    section_y = jnp.einsum("ij,ajl->ail", block, piece, precision=HIGHEST)
    piece = lax.all_gather(section_y, "gz", axis=2, tiled=True)
    place = jnp.arange(piece.shape[2], dtype=jnp.int32)
    col_pos = (place // wide_z * size_z + place % wide_z - 1).astype(jnp.float32)
    block = factor_block(own_z, col_pos, length_z)
    smooth = jnp.einsum("ij,abj->abi", block, piece, precision=HIGHEST)
    padded = with_halo(smooth, (("gx", 0), ("gy", 1), ("gz", 2)), 2)
    sample_index = tap_index(
        stencil_base[0] - anchor_x + 2,
        stencil_base[1] - anchor_y + 2,
        stencil_base[2] - anchor_z + 2,
        (size_y + 4) * (size_z + 4),
        size_z + 4,
        1,
    )
    picked = padded.reshape(-1)[sample_index]
    sampled = jnp.sum(stencil_weights * picked[:, :, None], axis=0).reshape(-1)
    image = live_mask * (sampled + noise * live_dir)
    norm_old, curvature = lax.psum(
        (jnp.sum(live_res * live_res), jnp.sum(live_dir * image)), ("gx", "gy", "gz")
    )
    step_size = norm_old / curvature
    new_residual = live_res - step_size * image
    norm_new = lax.psum(jnp.sum(new_residual * new_residual), ("gx", "gy", "gz"))
    new_iterate = live_mask * iterate + step_size * live_dir
    new_direction = new_residual + norm_new / norm_old * live_dir
    return (new_iterate, new_residual, new_direction)


def solution(mesh):
    return jax.shard_map(
        body,
        mesh=mesh,
        in_specs=(
            P(("gx", "gy", "gz")),
            P(("gx", "gy", "gz")),
            P(("gx", "gy", "gz")),
            P(("gx", "gy", "gz")),
            P(None, ("gx", "gy", "gz")),
            P(None, ("gx", "gy", "gz")),
            P(("gx", "gy", "gz")),
            P(),
        ),
        out_specs=(P(("gx", "gy", "gz")), P(("gx", "gy", "gz")), P(("gx", "gy", "gz"))),
        check_vma=False,
    )
```

profile of v0, /device:TPU:1, one launch (start us, length us, event | category | flops | bytes accessed | tf_op | source)
XLA Modules:
  0.0 908.4 jit_solution(16517070541006739412)
XLA Ops:
  8.1 1.5 fusion.85
  9.8 3.0 broadcast_multiply_fusion
  12.8 6.1 mul.208
  19.0 3.3 multiply_reduce_fusion.1
  22.4 44.3 %scatter_custom_fusion = f32[307195]{0:T(1024)} fusion(s32[8192]{0:T(1024)S(1)} %bitcast.80, f32[8192]{0:T(1024)S(1)} %bitcast.79, f32[]{:T(128)} %constant.90.clone.1), kind=kCustom, calls=%fused_computation.12 | custom fusion | flops 8192 | bytes 1228784 | tf_op jit(solution)/shard_map/scatter-add | solution.py:89
  66.7 3.0 reshape.330
  69.7 2.5 copy.21
  73.8 232.3 %all-gather.4.cloned.1.call-done = f32[560,67,131]{1,2,0:T(8,128)} async-done(((f32[35,67,131]{1,2,0:T(8,128)}), f32[560,67,131]{1,2,0:T(8,128)}) %all-gather.4.cloned.1.call-update) | async-done | bytes 19660496 | tf_op jit(solution)/shard_map/all_gather | solution.py:91
  306.1 35.1 %copy.31 = f32[560,67,131]{0,2,1:T(8,128)} copy(f32[560,67,131]{1,2,0:T(8,128)} %all-gather.4.cloned.1.call-done) | data formatting | bytes 39320960 | tf_op jit(solution)/shard_map/all_gather | solution.py:91
  341.2 32.3 %fusion.27 = f32[32,67,131]{2,0,1:T(8,128)} fusion(f32[560,67,131]{0,2,1:T(8,128)} %copy.31, f32[]{:T(128)S(6)} %sqrt.9, f32[]{:T(128)} %bitcast.1, f32[560]{0:T(1024)S(1)} %fusion.69, f32[32]{0:T(128)S(1)} %add_convert_fusion.2), kind=kOutput, calls=%fused_computation.35 | convolution fusion | flops 1887495680 | bytes 20786312 | tf_op jit(solution)/shard_map/ij,jkl->ikl/dot_general | solution.py:95
  374.5 86.7 %all-gather.6.cloned.1.call-done = f32[32,268,131]{2,0,1:T(8,128)} async-done(((f32[32,67,131]{2,0,1:T(8,128)}), f32[32,268,131]{2,0,1:T(8,128)}) %all-gather.6.cloned.1.call-update) | async-done | bytes 4493840 | tf_op jit(solution)/shard_map/all_gather | solution.py:96
  461.2 15.4 %fusion.4 = f32[32,64,131]{2,1,0:T(8,128)S(1)} fusion(f32[32,268,131]{2,0,1:T(8,128)} %all-gather.6.cloned.1.call-done, f32[]{:T(128)S(6)} %sqrt.10, f32[]{:T(128)} %bitcast.10, f32[268]{0:T(512)S(1)} %fusion.79, f32[64]{0:T(128)S(1)} %add_convert_fusion.1), kind=kOutput, calls=%fused_computation.10 | convolution fusion | flops 862899968 | bytes 5568312 | tf_op jit(solution)/shard_map/ij,ajl->ail/dot_general | solution.py:100
  476.6 2.6 copy.25
  479.9 157.9 %all-gather.8.cloned.1.call-done = f32[32,64,524]{1,0,2:T(8,128)} async-done(((f32[32,64,131]{1,0,2:T(8,128)}), f32[32,64,524]{1,0,2:T(8,128)}) %all-gather.8.cloned.1.call-update) | async-done | bytes 4292624 | tf_op jit(solution)/shard_map/all_gather | solution.py:101
  637.8 20.0 %fusion.2 = f32[32,64,128]{2,1,0:T(8,128)S(1)} fusion(f32[32,64,524]{1,0,2:T(8,128)} %all-gather.8.cloned.1.call-done, f32[]{:T(128)S(6)} %sqrt.11, f32[]{:T(128)} %bitcast.13, f32[524]{0:T(1024)S(1)} %fusion.67, f32[128]{0:T(128)S(1)} %add_convert_fusion), kind=kOutput, calls=%fused_computation.4 | convolution fusion | flops 1648696832 | bytes 5343800 | tf_op jit(solution)/shard_map/ij,abj->abi/dot_general | solution.py:105
  657.8 1.3 collective-permute-start
  660.4 4.5 collective-permute-done.1
  664.9 5.7 collective-permute-start.2
  670.6 1.9 collective-permute-start.3
  672.6 3.3 collective-permute-done.3
  676.1 1.5 fusion.83
  677.6 1.8 copy.27
  679.4 3.9 collective-permute-start.4
  683.8 1.6 collective-permute-start.5
  686.0 3.4 collective-permute-done.5
  689.4 1.6 copy.30
  691.0 4.1 pad_maximum_fusion
  695.1 3.4 reshape.331
  698.5 45.5 %gather_fusion = f32[8192]{0:T(1024)S(1)} fusion(f32[323136]{0:T(1024)S(1)} %reshape.331, s32[8192]{0:T(1024)S(1)} %fusion.49), kind=kCustom, calls=%fused_computation | custom fusion | bytes 98304 | tf_op jit(solution)/shard_map/gather | solution.py:115
  744.1 2.9 multiply_reduce_fusion
  747.7 76.5 %all-reduce = (f32[]{:T(128)}, f32[]{:T(128)}) all-reduce(f32[]{:T(128)} %get-tuple-element.4, f32[]{:T(128)} %get-tuple-element.3), channel_id=1, replica_groups=mesh['gx'=16,'gy'=4,'gz'=4] {'gx','gy','gz'}, use_global_device_ids=true, to_apply=%region_1.0 | all-reduce | flops 2 | bytes 16 | tf_op jit(solution)/shard_map/psum | solution.py:118
  826.2 73.5 %psum.23 = f32[]{:T(128)} all-reduce(f32[]{:T(128)} %get-tuple-element.7), channel_id=1, replica_groups=mesh['gx'=16,'gy'=4,'gz'=4] {'gx','gy','gz'}, use_global_device_ids=true, to_apply=%region_8.9 | all-reduce | flops 1 | bytes 8 | tf_op jit(solution)/shard_map/psum | solution.py:123
  (51 shorter events, 7.1 us)
Async XLA Ops:
  7.2 298.9 %all-gather.4.cloned.1.call-start = ((), (), s32[]{:S(2)}) async-start(), calls=%async_computation | async-start | bytes 41431040 | tf_op jit(solution)/shard_map/all_gather | solution.py:91
  12.8 6.1 copy-start
  12.8 6.1 copy-start.5
  69.7 2.8 copy-start.6
  72.2 388.9 %all-gather.6.cloned.1.call-start = ((), (), s32[]{:S(2)}) async-start(), calls=%async_computation.1 | async-start | bytes 10977280 | tf_op jit(solution)/shard_map/all_gather | solution.py:96
  373.5 264.3 %all-gather.8.cloned.1.call-start = ((), (), s32[]{:S(2)}) async-start(), calls=%async_computation.2 | async-start | bytes 10731520 | tf_op jit(solution)/shard_map/all_gather | solution.py:101
  657.8 2.6 collective-permute-start
  659.1 5.8 collective-permute-start.1
  664.9 7.7 collective-permute-start.2
  670.6 5.3 collective-permute-start.3
  679.4 6.0 collective-permute-start.4
  683.8 5.6 collective-permute-start.5
  744.1 2.9 copy-start.2
  744.1 2.9 copy-start.3
  744.1 157.0 %copy-start.4 = (f32[16384]{0:T(1024)S(1)}, f32[16384]{0:T(1024)}, u32[]{:S(2)}) copy-start(f32[16384]{0:T(1024)} %param.8) | copy-start | bytes 196612
  826.2 75.6 %copy-start.1 = (f32[16384]{0:T(1024)}, f32[16384]{0:T(1024)S(1)}, u32[]{:S(2)}) copy-start(f32[16384]{0:T(1024)S(1)} %get-tuple-element.8) | copy-start | bytes 196612
Sparse Core Ops, SparseCore 0:
  72.4 233.6 all-gather.3
  373.6 87.4 all-gather.5
  479.3 158.4 all-gather.7
where the time goes:
time: 910 us; the launch traced here: 908 us
  waiting for transfers between devices  488 us (54%)
  blocking collectives  150 us (16%)
  local copies, waits for them, and re-layouts  106 us (12%)
  matrix products  67.6 us (7%)
  other arithmetic  61.2 us (7%)
  between operations  18.8 us (2%)
  starting transfers between devices  16.3 us (2%)
    all_gather x1, waiting for transfers between devices, body(): piece = lax.all_gather(spread_grid, 'gx', axis=0, tiled=True)  232 us
    all_gather x1, waiting for transfers between devices, body(): piece = lax.all_gather(section_y, 'gz', axis=2, tiled=True)  158 us
    all_gather x1, waiting for transfers between devices, body(): piece = lax.all_gather(section_x, 'gy', axis=1, tiled=True)  86.7 us
    psum x1, blocking collectives, body(): lax.psum((jnp.sum(live_res * live_res), jnp.sum(live_dir * image)), ('gx'...  76.5 us
    psum x1, blocking collectives, body(): lax.psum(jnp.sum(new_residual * new_residual), ('gx', 'gy', 'gz'))  73.5 us
    gather x1, local copies, waits for them, and re-layouts, body(): picked = padded.reshape(-1)[sample_index]  45.5 us
    scatter-add x1, other arithmetic, body(): spread_grid.at[spread_index.reshape(-1)].add(tile_taps.reshape(-1))  44.3 us
    all_gather x1, local copies, waits for them, and re-layouts, body(): piece = lax.all_gather(spread_grid, 'gx', axis=0, tiled=True)  35.1 us
  transfers between devices with their start and end apart: 9, of which 6 were waited for; matrix products, arithmetic and copies ran while one was open for 0% of the time, Pallas kernels for 0%

commit v1 on v0

v1 whole, which is shorter than its diff:
```python
import functools

import jax
import jax.numpy as jnp
from jax import lax
from jax.experimental import pallas as pl
from jax.experimental.pallas import tpu as pltpu
from jax.sharding import PartitionSpec as P

F32 = jnp.float32
BF16 = jnp.bfloat16
LANES = 128
TILES = 128
NX, NY, NZ = 32, 64, 128
WX = NX + 3
TOP = 4
ROWS = 80
LIVE = 72
YT = LIVE // 8
SPARE, COPIES = 8, 20
STACKS = -(-WX * YT // COPIES)
MOMENT_STACKS, FIX_STACKS = -(-STACKS // 6), -(-STACKS // 3)
XROWS = 40
MESH = pl.DeviceIdType.MESH


def iota(shape, dim):
    return lax.broadcasted_iota(jnp.int32, shape, dim)


def full(value):
    return jnp.full((1, LANES), value, F32)


def decay(distance, length):
    return jnp.exp(-distance.astype(F32) / length)


def outgoing(kind, source, size, length):
    one = decay(full(1), length) - jnp.exp(full(1.0) / length)
    two = decay(full(2), length) - jnp.exp(full(2.0) / length)
    one, two = one[:, :1], two[:, :1]
    zero = jnp.zeros(source.shape, F32)
    if kind == 0:
        return decay(size + 1 - source, length)
    if kind == 1:
        return decay(source + 1, length)
    if kind == 2:
        return jnp.where(source == size, one, jnp.where(source == size + 1, two, zero))
    if kind == 3:
        return jnp.where(source == size + 1, one, zero)
    if kind == 4:
        return jnp.where(source == -1, two, jnp.where(source == 0, one, zero))
    return jnp.where(source == -1, one, zero)


def incoming(kind, cell, size, length):
    if kind == 0:
        return decay(cell - 1, length)
    if kind == 1:
        return decay(size - 1 - cell, length)
    target = (-1, 0, size + 1, size)[kind - 2]
    return jnp.where(cell == target, 1.0, 0.0).astype(F32)


def tile_weights(w8, low):
    along_y = jnp.where(low, pltpu.roll(w8, 4, 0), w8)
    first = jnp.where(low, w8[0:1], w8[1:2]) * along_y
    second = jnp.where(low, w8[2:3], w8[3:4]) * along_y
    return first, second, along_y


def spread_kernel(count, base, reach, w, direction, residual, grid, live_dir, live_res, live, table):
    anchor_x = lax.axis_index("gx") * NX
    anchor_y = lax.axis_index("gy") * NY
    anchor_z = lax.axis_index("gz") * NZ
    length = reach[2] * float(NZ)
    scale = 1.0 / (
        jnp.sqrt(full(reach[0] * float(NX))) * jnp.sqrt(full(reach[1] * float(NY))) * jnp.sqrt(full(length))
    )
    source = iota((136, LANES), 0) - 1
    lane = iota((136, LANES), 1)
    table[0] = decay(jnp.abs(lane - 1 - source), length) * scale
    second = jnp.where(lane < 3, decay(jnp.abs(lane + NZ - 1 - source), length), 0.0)
    for kind in range(6):
        start = SPARE + COPIES * kind
        inside = (lane >= start) & (lane < start + COPIES)
        second = jnp.where(inside, outgoing(kind, source, NZ, length), second)
    table[1] = second * scale

    def clear(x, carry):
        for half in range(2):
            grid[x, half] = jnp.zeros((ROWS, LANES), F32)
        return carry

    lax.fori_loop(0, WX, clear, 0)
    low = iota((8, LANES), 0) < 4
    slot = iota((1, LANES), 1)

    def tile(t, carry):
        at = pl.ds(pl.multiple_of(t * LANES, LANES), LANES)
        w8 = w[0:8, at]
        mask = slot < count[t]
        values = jnp.where(mask, direction[pl.ds(t, 1), :], 0.0)
        live_dir[pl.ds(t, 1), :] = values
        live_res[pl.ds(t, 1), :] = jnp.where(mask, residual[pl.ds(t, 1), :], 0.0)
        live[pl.ds(t, 1), :] = jnp.where(mask, 1.0, 0.0)
        first, second, _ = tile_weights(w8, low)
        x0 = base[0, t] - anchor_x + 1
        y0 = base[1, t] - anchor_y + 1 + TOP
        z0 = base[2, t] - anchor_z + 1
        parts = [[None, None], [None, None]]
        for e in range(4):
            along_z = w[8 + e : 9 + e, at] * values
            row = [table[half, pl.ds(z0 + e, 1), :] for half in range(2)]
            for pair, product in enumerate((first, second)):
                taps = jnp.sum(product * along_z, axis=1, keepdims=True)
                for half in range(2):
                    term = taps * row[half]
                    parts[pair][half] = term if e == 0 else parts[pair][half] + term
        for a in range(4):
            start = y0 if a % 2 == 0 else y0 - 4
            keep = low if a % 2 == 0 else jnp.logical_not(low)
            for half in range(2):
                spot = (x0 + a, half, pl.ds(start, 8), slice(None))
                grid[spot] = grid[spot] + jnp.where(keep, parts[a // 2][half], 0.0)
        return carry

    lax.fori_loop(0, TILES, tile, 0, unroll=2)


def partner(axis, me, offset, count):
    return {axis: lax.rem(me + offset, count)}


def solve_kernel(
    sizes,
    base,
    reach,
    grid,
    live_dir,
    live_res,
    live,
    noise,
    w_hbm,
    image,
    sums,
    w,
    forward,
    smooth,
    basis,
    pick_z,
    pick_x,
    z_moment,
    z_fix,
    z_moment_in,
    z_fix_in,
    y_out,
    y_moment_in,
    y_fix_in,
    x_moment,
    x_fix,
    x_fix_in,
    x_chunk_in,
    x_prefix,
    x_far,
    sampled,
    sum_out,
    sum_in_x,
    sum_mid,
    sum_in_yz,
    w_sem,
    z_sem,
    z_fix_sem,
    y_sem,
    y_fix_sem,
    x_fix_sem,
    x1_send,
    x1_recv,
    x2_send,
    x2_recv,
    sx_sem,
    syz_sem,
):
    n_gx, n_gy, n_gz = sizes
    n_yz = n_gy * n_gz
    px, py, pz = lax.axis_index("gx"), lax.axis_index("gy"), lax.axis_index("gz")
    pyz = py * n_gz + pz
    length_x, length_y, length_z = reach[0] * float(NX), reach[1] * float(NY), reach[2] * float(NZ)

    def yz_partner(offset):
        other = lax.rem(pyz + offset, n_yz)
        return {"gy": other // n_gz, "gz": lax.rem(other, n_gz)}

    barrier = pltpu.get_barrier_semaphore()
    for k in range(1, n_gx):
        pl.semaphore_signal(barrier, inc=1, device_id=partner("gx", px, k, n_gx), device_id_type=MESH)
    for k in range(1, n_yz):
        pl.semaphore_signal(barrier, inc=1, device_id=yz_partner(k), device_id_type=MESH)

    w_copy = pltpu.make_async_copy(w_hbm, w, w_sem)
    w_copy.start()

    def remote(src, dst, send, recv, device):
        return pltpu.make_async_remote_copy(
            src_ref=src, dst_ref=dst, send_sem=send, recv_sem=recv, device_id=device, device_id_type=MESH
        )

    sub = iota((8, LANES), 0)
    lane = iota((8, LANES), 1)
    low = sub < 4
    copy_of = jnp.where(lane < SPARE, -1, lax.rem(lane - SPARE + COPIES, COPIES))

    row = iota((96, 3 * ROWS), 0)
    col = iota((96, 3 * ROWS), 1)
    part = col // ROWS
    source = col - part * ROWS - TOP - 1
    cell = row - TOP - 1
    entry = jnp.where((cell >= -1) & (cell <= NY + 1), decay(jnp.abs(cell - source), length_y), 0.0)
    for kind in range(6):
        entry = jnp.where(row == ROWS + kind, outgoing(kind, source, NY, length_y), entry)
    entry = jnp.where((source >= -1) & (source <= NY + 1), entry, 0.0)
    entry_high = entry.astype(BF16).astype(F32)
    basis[...] = jnp.where(part == 1, entry - entry_high, entry_high).astype(BF16)
    cell = iota((136, LANES), 0) - 1
    wide = iota((136, LANES), 1)
    pick_z[0] = jnp.where(wide == cell + 1, 1.0, 0.0).astype(F32)
    picked = jnp.where((wide < 3) & (wide + NZ - 1 == cell), 1.0, 0.0).astype(F32)
    for kind in range(6):
        start = SPARE + COPIES * kind
        picked = jnp.where((wide >= start) & (wide < start + COPIES), incoming(kind, cell, NZ, length_z), picked)
    pick_z[1] = picked
    cell = iota((XROWS, LANES), 0) - 1
    for kind in range(2):
        pick_x[kind] = incoming(kind, cell, NX, length_x)
    for side in range(2):
        for half in range(2):
            x_far[side, half, LIVE:ROWS, :] = jnp.zeros((ROWS - LIVE, LANES), F32)

    def mix(pos, count, size, length, k):
        from_left = pos >= k
        left = jnp.where(from_left, jnp.exp(full(-float(size * (k - 1))) / length), 0.0)
        right = jnp.where(from_left, 0.0, jnp.exp(full(-float(size * (count - k - 1))) / length))
        return left, right

    stacks = [None] * STACKS
    for j in range(WX * YT):
        x, yt = divmod(j, YT)
        stack, copy = divmod(j, COPIES)
        value = grid[x, 1, 8 * yt : 8 * yt + 8, :]
        stacks[stack] = value if copy == 0 else jnp.where(copy_of == copy, value, stacks[stack])
    for kind in range(2):
        for group in range(MOMENT_STACKS):
            total = jnp.zeros((8, LANES), F32)
            for i, stack in enumerate(range(6 * group, min(6 * group + 6, STACKS))):
                shift = (COPIES * i - SPARE - COPIES * kind) % LANES
                moved = pltpu.roll(stacks[stack], shift, 1) if shift else stacks[stack]
                total = jnp.where((lane >= COPIES * i) & (lane < COPIES * (i + 1)), moved, total)
            z_moment[kind, group] = total
        for group in range(FIX_STACKS):
            total = jnp.zeros((8, LANES), F32)
            for i, stack in enumerate(range(3 * group, min(3 * group + 3, STACKS))):
                shift = (2 * COPIES * i - SPARE - 2 * COPIES * (kind + 1)) % LANES
                moved = pltpu.roll(stacks[stack], shift, 1) if shift else stacks[stack]
                total = jnp.where((lane >= 2 * COPIES * i) & (lane < 2 * COPIES * (i + 1)), moved, total)
            z_fix[kind, group] = total

    pl.semaphore_wait(barrier, n_gx - 1 + n_yz - 1)

    def exchange(axis, pos, count, moment, moment_in, fix, fix_in, sem, fix_sem):
        copies = []
        for k in range(1, count):
            way = jnp.where(pos + k < count, 0, 1)
            copy = remote(
                moment.at[way], moment_in.at[k - 1], sem.at[0, k - 1], sem.at[1, k - 1], partner(axis, pos, k, count)
            )
            copy.start()
            copies.append(copy)
        if count > 1:
            right = remote(
                fix.at[0], fix_in.at[0], fix_sem.at[0, 0], fix_sem.at[1, 0], partner(axis, pos, 1, count)
            )
            left = remote(
                fix.at[1], fix_in.at[1], fix_sem.at[0, 1], fix_sem.at[1, 1], partner(axis, pos, count - 1, count)
            )
            pl.when(pos + 1 < count)(right.start)
            pl.when(pos > 0)(left.start)

        def wait_fix():
            if count > 1:
                pl.when(pos > 0)(right.wait_recv)
                pl.when(pos + 1 < count)(left.wait_recv)

        def wait_moment():
            for copy in copies:
                copy.wait_recv()

        def wait_send():
            for copy in copies:
                copy.wait_send()
            if count > 1:
                pl.when(pos + 1 < count)(right.wait_send)
                pl.when(pos > 0)(left.wait_send)

        return wait_moment, wait_fix, wait_send

    z_wait, z_wait_fix, z_done = exchange(
        "gz", pz, n_gz, z_moment, z_moment_in, z_fix, z_fix_in, z_sem, z_fix_sem
    )
    z_wait()
    z_wait_fix()
    mixed = [[jnp.zeros((8, LANES), F32) for _ in range(MOMENT_STACKS)] for _ in range(2)]
    for k in range(1, n_gz):
        weights = mix(pz, n_gz, NZ, length_z, k)
        for group in range(MOMENT_STACKS):
            got = z_moment_in[k - 1, group]
            for side in range(2):
                mixed[side][group] = mixed[side][group] + weights[side] * got
    fixes = [[jnp.where(pz > 0, z_fix_in[0, group], 0.0) for group in range(FIX_STACKS)]]
    fixes.append([jnp.where(pz + 1 < n_gz, z_fix_in[1, group], 0.0) for group in range(FIX_STACKS)])
    for stack in range(STACKS):
        total = jnp.zeros((8, LANES), F32)
        for kind in range(2):
            group, i = divmod(stack, 6)
            start = SPARE + COPIES * kind
            shift = (start - COPIES * i) % LANES
            moved = pltpu.roll(mixed[kind][group], shift, 1) if shift else mixed[kind][group]
            total = jnp.where((lane >= start) & (lane < start + COPIES), moved, total)
            group, i = divmod(stack, 3)
            start = SPARE + 2 * COPIES * (kind + 1)
            shift = (start - 2 * COPIES * i) % LANES
            moved = pltpu.roll(fixes[kind][group], shift, 1) if shift else fixes[kind][group]
            total = jnp.where((lane >= start) & (lane < start + 2 * COPIES), moved, total)
        for copy in range(COPIES):
            j = stack * COPIES + copy
            if j < WX * YT:
                x, yt = divmod(j, YT)
                spot = slice(8 * yt, 8 * yt + 8)
                value = jnp.where(copy_of == copy, total, 0.0)
                forward[x, 1, spot, :] = jnp.where(lane < SPARE, grid[x, 1, spot, :], value)
    for x in range(WX):
        forward[x, 1, LIVE:ROWS, :] = jnp.zeros((ROWS - LIVE, LANES), F32)

    def contract(x, carry):
        for half in range(2):
            values = (grid, forward)[half][x, half]
            high = values.astype(BF16)
            rest = (values - high.astype(F32)).astype(BF16)
            stacked = jnp.concatenate([high, high, rest], axis=0)
            result = jnp.dot(basis[...], stacked, preferred_element_type=F32)
            smooth[x, half] = result[:ROWS]
            for kind in range(6):
                y_out[kind // 2, kind % 2, half, pl.ds(x, 1), :] = result[ROWS + kind : ROWS + kind + 1]
        return carry

    lax.fori_loop(0, WX, contract, 0)
    y_wait, y_wait_fix, y_done = exchange(
        "gy", py, n_gy, y_out.at[0], y_moment_in, y_out.at[pl.ds(1, 2)], y_fix_in, y_sem, y_fix_sem
    )
    y_wait()
    y_wait_fix()
    far_y = []
    for half in range(2):
        totals = [jnp.zeros((XROWS, LANES), F32) for _ in range(2)]
        for k in range(1, n_gy):
            weights = mix(py, n_gy, NY, length_y, k)
            got = y_moment_in[k - 1, half]
            totals = [total + weight * got for total, weight in zip(totals, weights)]
        far_y.append(totals)
    for half in range(2):
        for side in range(2):
            y_moment_in[side, half] = far_y[half][side]
    has_left, has_right = py > 0, py + 1 < n_gy

    step_x = jnp.exp(full(-1.0) / length_x)
    fix_one = step_x - jnp.exp(full(1.0) / length_x)
    fix_two = jnp.exp(full(-2.0) / length_x) - jnp.exp(full(2.0) / length_x)

    def scan(yt, carry):
        rows = pl.ds(pl.multiple_of(yt * 8, 8), 8)
        cell = iota((8, LANES), 0) + yt * 8 - TOP - 1
        from_left = incoming(0, cell, NY, length_y)
        from_right = incoming(1, cell, NY, length_y)
        for half in range(2):
            state = None
            ends = {}
            for x in range(WX):
                value = smooth[x, half, rows, :]
                value = value + from_left * y_moment_in[0, half, x : x + 1, :]
                value = value + from_right * y_moment_in[1, half, x : x + 1, :]
                left = jnp.where(has_left, y_fix_in[0, :, half, x : x + 1, :], 0.0)
                right = jnp.where(has_right, y_fix_in[1, :, half, x : x + 1, :], 0.0)
                value = value + jnp.where(cell == -1, left[0], jnp.where(cell == 0, left[1], 0.0))
                value = value + jnp.where(cell == NY + 1, right[0], jnp.where(cell == NY, right[1], 0.0))
                smooth[x, half, rows, :] = value
                state = value if x == 0 else value + step_x * state
                forward[x, half, rows, :] = state
                if x < 2 or x >= WX - 2:
                    ends[x] = value
            x_moment[0, half, rows, :] = state
            x_fix[0, 0, half, rows, :] = ends[WX - 2] * fix_one + ends[WX - 1] * fix_two
            x_fix[0, 1, half, rows, :] = ends[WX - 1] * fix_one
            x_fix[1, 0, half, rows, :] = ends[0] * fix_two + ends[1] * fix_one
            x_fix[1, 1, half, rows, :] = ends[0] * fix_one
            state = jnp.zeros((8, LANES), F32)
            for x in reversed(range(WX)):
                value = smooth[x, half, rows, :]
                smooth[x, half, rows, :] = forward[x, half, rows, :] + state
                if x == 0:
                    x_moment[1, half, rows, :] = state + value
                state = step_x * (state + value)
        return carry

    lax.fori_loop(0, YT, scan, 0)

    right = left = None
    if n_gx > 1:
        right = remote(x_fix.at[0], x_fix_in.at[0], x_fix_sem.at[0, 0], x_fix_sem.at[1, 0], partner("gx", px, 1, n_gx))
        left = remote(
            x_fix.at[1], x_fix_in.at[1], x_fix_sem.at[0, 1], x_fix_sem.at[1, 1], partner("gx", px, n_gx - 1, n_gx)
        )

    def chunk(index):
        return pl.ds(pl.multiple_of(index * 8, 8), 8)

    first_sends = []
    for c in range(YT):
        copy = remote(x_moment.at[:, :, chunk(c), :], x_chunk_in.at[px], x1_send.at[c], x1_recv.at[px], {"gx": c})
        first_sends.append((px != c, copy))
        pl.when(px != c)(copy.start)
    if n_gx > 1:
        pl.when(px + 1 < n_gx)(right.start)
        pl.when(px > 0)(left.start)

    @pl.when(px < YT)
    def _():
        x_chunk_in[px] = x_moment[:, :, chunk(px), :]
        for p in range(n_gx):
            copy = remote(
                x_moment.at[:, :, chunk(0), :], x_chunk_in.at[p], x1_send.at[0], x1_recv.at[p], {"gx": p}
            )
            pl.when(px != p)(copy.wait_recv)
        ratio = jnp.exp(full(-float(NX)) / length_x)
        for side, order in enumerate((range(n_gx), reversed(range(n_gx)))):
            total = [jnp.zeros((8, LANES), F32) for _ in range(2)]
            for q in order:
                for half in range(2):
                    x_prefix[q, side, half] = total[half]
                    total[half] = total[half] * ratio + x_chunk_in[q, side, half]
        for q in range(n_gx):
            copy = remote(x_prefix.at[q], x_far.at[:, :, chunk(px), :], x2_send.at[q], x2_recv.at[px], {"gx": q})
            pl.when(px != q)(copy.start)
        x_far[:, :, chunk(px), :] = x_prefix[px]

    if n_gx > 1:
        pl.when(px > 0)(right.wait_recv)
        pl.when(px + 1 < n_gx)(left.wait_recv)
    for half in range(2):
        for kind, x in enumerate((0, 1)):
            smooth[x, half, 0:LIVE, :] += jnp.where(px > 0, x_fix_in[0, kind, half], 0.0)
        for kind, x in enumerate((WX - 1, WX - 2)):
            smooth[x, half, 0:LIVE, :] += jnp.where(px + 1 < n_gx, x_fix_in[1, kind, half], 0.0)
    w_copy.wait()

    def tile_spot(t):
        at = pl.ds(pl.multiple_of(t * LANES, LANES), LANES)
        x0 = jnp.clip(base[0, t] - px * NX + 1, 0, NX - 1)
        y0 = jnp.clip(base[1, t] - py * NY + 1, 0, NY - 1) + TOP
        z0 = jnp.clip(base[2, t] - pz * NZ + 1, 0, NZ - 1)
        return at, x0, y0, z0

    def gather(rows, weights, at, z0):
        total = None
        for e in range(4):
            pick = [pick_z[half, pl.ds(z0 + e, 1), :] for half in range(2)]
            inner = None
            for cells, weight in zip(rows, weights):
                taps = jnp.sum(cells[0] * pick[0] + cells[1] * pick[1], axis=1, keepdims=True)
                inner = weight * taps if inner is None else inner + weight * taps
            inner = inner * w[8 + e : 9 + e, at]
            total = inner if e == 0 else total + inner
        return jnp.sum(total, axis=0, keepdims=True)

    def near(t, carry):
        at, x0, y0, z0 = tile_spot(t)
        first, second, _ = tile_weights(w[0:8, at], low)
        rows = [
            [
                jnp.where(
                    low, smooth[x0 + a, half, pl.ds(y0, 8), :], smooth[x0 + a + 1, half, pl.ds(y0 - 4, 8), :]
                )
                for half in range(2)
            ]
            for a in (0, 2)
        ]
        sampled[pl.ds(t, 1), :] = gather(rows, (first, second), at, z0)
        return carry

    lax.fori_loop(0, TILES, near, 0, unroll=2)

    for c in range(YT):
        copy = remote(x_prefix.at[0], x_far.at[:, :, chunk(c), :], x2_send.at[0], x2_recv.at[c], {"gx": c})
        pl.when(px != c)(copy.wait_recv)

    def far(t, carry):
        at, x0, y0, z0 = tile_spot(t)
        w8 = w[0:8, at]
        _, _, along_y = tile_weights(w8, low)
        along_x = []
        for side in range(2):
            total = None
            for a in range(4):
                term = w8[a : a + 1] * pick_x[side, pl.ds(x0 + a, 1), :]
                total = term if a == 0 else total + term
            along_x.append(total)
        weight = jnp.where(low, along_x[0], along_x[1]) * along_y
        rows = [jnp.where(low, x_far[0, half, pl.ds(y0, 8), :], x_far[1, half, pl.ds(y0 - 4, 8), :]) for half in range(2)]
        sampled[pl.ds(t, 1), :] += gather([rows], [weight], at, z0)
        return carry

    lax.fori_loop(0, TILES, far, 0, unroll=2)

    value = live[...] * (sampled[...] + noise[...] * live_dir[...])
    image[...] = value
    pairs = (
        (live_res[...], live_res[...]),
        (live_dir[...], value),
        (live_res[...], value),
        (value, value),
    )
    sum_out[...] = jnp.concatenate(
        [jnp.sum(a * b, axis=0, keepdims=True) for a, b in pairs] + [jnp.zeros((4, LANES), F32)], axis=0
    )
    last = []
    for k in range(1, n_gx):
        copy = remote(sum_out, sum_in_x.at[k - 1], sx_sem.at[0, k - 1], sx_sem.at[1, k - 1], partner("gx", px, k, n_gx))
        copy.start()
        last.append(copy)
    total = sum_out[...]
    for k in range(1, n_gx):
        last[k - 1].wait_recv()
        total = total + sum_in_x[k - 1]
    sum_mid[...] = total
    more = []
    for k in range(1, n_yz):
        copy = remote(sum_mid, sum_in_yz.at[k - 1], syz_sem.at[0, k - 1], syz_sem.at[1, k - 1], yz_partner(k))
        copy.start()
        more.append(copy)
    for k in range(1, n_yz):
        more[k - 1].wait_recv()
        total = total + sum_in_yz[k - 1]
    sums[...] = total

    for copy in last + more:
        copy.wait_send()
    z_done()
    y_done()
    if n_gx > 1:
        pl.when(px + 1 < n_gx)(right.wait_send)
        pl.when(px > 0)(left.wait_send)
    for sent, copy in first_sends:
        pl.when(sent)(copy.wait_send)

    @pl.when(px < YT)
    def _():
        for q in range(n_gx):
            copy = remote(x_prefix.at[q], x_far.at[:, :, chunk(px), :], x2_send.at[q], x2_recv.at[px], {"gx": q})
            pl.when(px != q)(copy.wait_send)


def update_kernel(sums, iterate, live, live_dir, live_res, image, new_iterate, new_residual, new_direction):
    def total(row):
        return jnp.sum(sums[row : row + 1, :], axis=1, keepdims=True)

    norm_old, curvature, cross, square = total(0), total(1), total(2), total(3)
    step = norm_old / curvature
    norm_new = norm_old + step * (step * square - 2.0 * cross)
    held = live_res[...] - step * image[...]
    new_iterate[...] = live[...] * iterate[...] + step * live_dir[...]
    new_residual[...] = held
    new_direction[...] = held + norm_new / norm_old * live_dir[...]


def body(sizes, iterate, residual, direction, noise, stencil_base, interp_weights, tile_counts, reach):
    n_gx, n_gy, n_gz = sizes
    n_yz = n_gy * n_gz
    square = (TILES, LANES)
    in_vmem = pl.BlockSpec(memory_space=pltpu.VMEM)
    in_smem = pl.BlockSpec(memory_space=pltpu.SMEM)

    def keep(x):
        return pltpu.with_memory_space_constraint(x, pltpu.VMEM)

    grid, live_dir, live_res, live = pl.pallas_call(
        spread_kernel,
        out_shape=[pltpu.VMEM((WX, 2, ROWS, LANES), F32)] + [pltpu.VMEM(square, F32)] * 3,
        in_specs=[in_smem] * 3 + [in_vmem] * 3,
        out_specs=[in_vmem] * 4,
        scratch_shapes=[pltpu.VMEM((2, 136, LANES), F32)],
        compiler_params=pltpu.CompilerParams(vmem_limit_bytes=16 << 20),
        name="spread",
    )(tile_counts, stencil_base, reach, interp_weights, direction.reshape(square), residual.reshape(square))

    dma = pltpu.SemaphoreType.DMA
    image, sums = pl.pallas_call(
        functools.partial(solve_kernel, sizes),
        out_shape=[pltpu.VMEM(square, F32), pltpu.VMEM((8, LANES), F32)],
        in_specs=[in_smem] * 2 + [in_vmem] * 5 + [pl.BlockSpec(memory_space=pl.ANY)],
        out_specs=[in_vmem] * 2,
        scratch_shapes=[
            pltpu.VMEM((12, TILES * LANES), F32),
            pltpu.VMEM((WX, 2, ROWS, LANES), F32),
            pltpu.VMEM((WX, 2, ROWS, LANES), F32),
            pltpu.VMEM((96, 3 * ROWS), BF16),
            pltpu.VMEM((2, 136, LANES), F32),
            pltpu.VMEM((2, XROWS, LANES), F32),
            pltpu.VMEM((2, MOMENT_STACKS, 8, LANES), F32),
            pltpu.VMEM((2, FIX_STACKS, 8, LANES), F32),
            pltpu.VMEM((3, MOMENT_STACKS, 8, LANES), F32),
            pltpu.VMEM((2, FIX_STACKS, 8, LANES), F32),
            pltpu.VMEM((3, 2, 2, XROWS, LANES), F32),
            pltpu.VMEM((3, 2, XROWS, LANES), F32),
            pltpu.VMEM((2, 2, 2, XROWS, LANES), F32),
            pltpu.VMEM((2, 2, LIVE, LANES), F32),
            pltpu.VMEM((2, 2, 2, LIVE, LANES), F32),
            pltpu.VMEM((2, 2, 2, LIVE, LANES), F32),
            pltpu.VMEM((n_gx, 2, 2, 8, LANES), F32),
            pltpu.VMEM((n_gx, 2, 2, 8, LANES), F32),
            pltpu.VMEM((2, 2, ROWS, LANES), F32),
            pltpu.VMEM(square, F32),
            pltpu.VMEM((8, LANES), F32),
            pltpu.VMEM((15, 8, LANES), F32),
            pltpu.VMEM((8, LANES), F32),
            pltpu.VMEM((15, 8, LANES), F32),
            dma,
            dma((2, 3)),
            dma((2, 2)),
            dma((2, 3)),
            dma((2, 2)),
            dma((2, 2)),
            dma((YT,)),
            dma((n_gx,)),
            dma((n_gx,)),
            dma((YT,)),
            dma((2, 15)),
            dma((2, 15)),
        ],
        compiler_params=pltpu.CompilerParams(
            collective_id=0, has_side_effects=True, vmem_limit_bytes=24 << 20
        ),
        name="solve",
    )(
        stencil_base,
        reach,
        keep(grid),
        keep(live_dir),
        keep(live_res),
        keep(live),
        noise.reshape(square),
        interp_weights,
    )

    outs = pl.pallas_call(
        update_kernel,
        out_shape=[jax.ShapeDtypeStruct(square, F32)] * 3,
        in_specs=[in_vmem] * 6,
        out_specs=[in_vmem] * 3,
        name="update",
    )(keep(sums), iterate.reshape(square), keep(live), keep(live_dir), keep(live_res), keep(image))
    return tuple(out.reshape(-1) for out in outs)


def solution(mesh):
    sizes = tuple(mesh.shape[axis] for axis in ("gx", "gy", "gz"))
    lines = P(("gx", "gy", "gz"))
    return jax.shard_map(
        functools.partial(body, sizes),
        mesh=mesh,
        in_specs=(lines, lines, lines, lines, P(None, ("gx", "gy", "gz")), P(None, ("gx", "gy", "gz")), lines, P()),
        out_specs=(lines, lines, lines),
        check_vma=False,
    )
```

time: 910 us -> 80.7 us (0.09)
  waiting for transfers between devices: 488 us -> 0 us
  blocking collectives: 150 us -> 0 us
  local copies, waits for them, and re-layouts: 106 us -> 8.28 us
  Pallas kernels: 0 us -> 71.4 us
  matrix products: 67.6 us -> 0 us
  other arithmetic: 61.2 us -> 0 us
  between operations: 18.8 us -> 0.67 us
  starting transfers between devices: 16.3 us -> 0 us
    all_gather x3 -> x0, waiting for transfers between devices: 477 us -> none  [the longest x1 232 us: body(): piece = lax.all_gather(spread_grid, 'gx', axis=0, tiled=True)]
    psum x2 -> x0, blocking collectives: 150 us -> none  [the longest x1 76.5 us: body(): lax.psum((jnp.sum(live_res * live_res), jnp.sum(live_dir * image)), ('gx'...]
    pallas_call x0 -> x3, Pallas kernels: none -> 71.4 us  [the longest x1 62.2 us: body(): pl.pallas_call(functools.partial(solve_kernel, sizes), out_shape=[pltpu.V...]
    dot_general x3 -> x0, matrix products: 67.6 us -> none  [the longest x1 32.3 us: body(): section_x = jnp.einsum('ij,jkl->ikl', block, piece, precision=HIGHEST)]
    gather x1 -> x0, local copies, waits for them, and re-layouts: 45.5 us -> none  [body(): picked = padded.reshape(-1)[sample_index]]
    scatter-add x1 -> x0, other arithmetic: 44.3 us -> none  [body(): spread_grid.at[spread_index.reshape(-1)].add(tile_taps.reshape(-1))]
    all_gather x1 -> x0, local copies, waits for them, and re-layouts: 35.1 us -> none  [body(): piece = lax.all_gather(spread_grid, 'gx', axis=0, tiled=True)]
    ppermute x6 -> x0, starting transfers between devices: 15.8 us -> none  [the longest x3 10.9 us: with_halo(): lax.ppermute(tail, axis, [(i, (i + 1) % count) for i in range(ends)])]
  transfers between devices with their start and end apart: 9 -> 0, of which waited for: 6 -> 0; matrix products, arithmetic and copies ran while one was open for 0% -> 0% of each run, Pallas kernels for 0% -> 0%
where the time goes in v1:
time: 80.7 us; the launch traced here: 80.3 us
  Pallas kernels  71.4 us (88%)
  local copies, waits for them, and re-layouts  8.28 us (10%)
    pallas_call x1, Pallas kernels, body(): pl.pallas_call(functools.partial(solve_kernel, sizes), out_shape=[pltpu.V...  62.2 us
    unnamed x20, local copies, waits for them, and re-layouts  8.28 us
    pallas_call x1, Pallas kernels, body(): pl.pallas_call(spread_kernel, out_shape=[pltpu.VMEM((WX, 2, ROWS, LANES),...  7.53 us

profile of v1, /device:TPU:1, one launch (start us, length us, event | category | flops | bytes accessed | tf_op | source)
XLA Modules:
  0.0 80.3 jit_solution(9638318234437131156)
XLA Ops:
  0.6 0.0 copy-start
  0.6 1.2 %copy-done = f32[12,16384]{1,0:T(8,128)S(1)} copy-done((f32[12,16384]{1,0:T(8,128)S(1)}, f32[12,16384]{1,0:T(8,128)}, u32[]{:S(2)}) %copy-start) | copy-done | bytes 786456
  1.9 0.0 copy-start.3
  1.9 0.8 %copy-done.3 = f32[16384]{0:T(1024)S(1)} copy-done((f32[16384]{0:T(1024)S(1)}, f32[16384]{0:T(1024)}, u32[]{:S(2)}) %copy-start.3) | copy-done | bytes 65560
  2.7 0.0 copy-start.4
  2.7 0.8 %copy-done.4 = f32[16384]{0:T(1024)S(1)} copy-done((f32[16384]{0:T(1024)S(1)}, f32[16384]{0:T(1024)}, u32[]{:S(2)}) %copy-start.4) | copy-done | bytes 65560
  3.5 0.0 copy-start.5
  3.5 0.7 copy-done.5
  4.2 0.0 copy-start.7
  4.2 0.7 copy-done.7
  4.9 0.0 copy-start.9
  4.9 0.7 copy-done.9
  5.5 7.5 %spread.1 = (f32[35,2,80,128]{3,2,1,0:T(8,128)S(1)}, f32[128,128]{1,0:T(8,128)S(1)}, f32[128,128]{1,0:T(8,128)S(1)}, f32[128,128]{1,0:T(8,128)S(1)}) custom-call(s32[128]{0:T(128)S(1)} %copy-done.9, s32[3,128]{1,0:T(4,128)S(1)} %copy-done.5, f32[3]{0:T(128)S(1)} %copy-done.7, f32[12,16384]{1,0:T(8,128)S(1)} %copy-done, f32[128,128]{1,0:T(8,128)S(1)} %bitcast.8, ...), custom_call_target="tpu_custom_call" | custom-call | tf_op jit(solution)/shard_map/spread/pallas_call | solution.py:594
  13.1 0.0 copy-start.1
  13.1 1.2 %copy-done.1 = f32[12,16384]{1,0:T(8,128)S(1)} copy-done((f32[12,16384]{1,0:T(8,128)S(1)}, f32[12,16384]{1,0:T(8,128)}, u32[]{:S(2)}) %copy-start.1) | copy-done | bytes 786456
  14.3 0.0 copy-start.2
  14.3 0.8 %copy-done.2 = f32[16384]{0:T(1024)S(1)} copy-done((f32[16384]{0:T(1024)S(1)}, f32[16384]{0:T(1024)}, u32[]{:S(2)}) %copy-start.2) | copy-done | bytes 65560
  15.1 0.0 copy-start.6
  15.1 0.7 copy-done.6
  15.8 0.0 copy-start.8
  15.8 0.7 copy-done.8
  16.5 62.2 %solve.1 = (f32[128,128]{1,0:T(8,128)S(1)}, f32[8,128]{1,0:T(8,128)S(1)}) custom-call(s32[3,128]{1,0:T(4,128)S(1)} %copy-done.6, f32[3]{0:T(128)S(1)} %copy-done.8, f32[35,2,80,128]{3,2,1,0:T(8,128)S(1)} %get-tuple-element.12.grid, f32[128,128]{1,0:T(8,128)S(1)} %get-tuple-element.13.live_dir, f32[128,128]{1,0:T(8,128)S(1)} %get-tuple-element.14.live_res, ...), custom_call_target="tpu_custom_call" | custom-call | tf_op jit(solution)/shard_map/solve/pallas_call | solution.py:605
  78.7 1.6 %update.1 = (f32[128,128]{1,0:T(8,128)}, f32[128,128]{1,0:T(8,128)}, f32[128,128]{1,0:T(8,128)}) custom-call(f32[8,128]{1,0:T(8,128)S(1)} %get-tuple-element.16.sums, f32[128,128]{1,0:T(8,128)} %bitcast.10, f32[128,128]{1,0:T(8,128)S(1)} %get-tuple-element.15.live, f32[128,128]{1,0:T(8,128)S(1)} %get-tuple-element.13.live_dir, ...), custom_call_target="tpu_custom_call" | custom-call | tf_op jit(solution)/shard_map/update/pallas_call | solution.py:663
Async XLA Ops:
  0.6 1.2 %copy-start = (f32[12,16384]{1,0:T(8,128)S(1)}, f32[12,16384]{1,0:T(8,128)}, u32[]{:S(2)}) copy-start(f32[12,16384]{1,0:T(8,128)} %w_hbm.1) | copy-start | bytes 2359300
  1.9 0.8 %copy-start.3 = (f32[16384]{0:T(1024)S(1)}, f32[16384]{0:T(1024)}, u32[]{:S(2)}) copy-start(f32[16384]{0:T(1024)} %param.10) | copy-start | bytes 196612
  2.7 0.8 %copy-start.4 = (f32[16384]{0:T(1024)S(1)}, f32[16384]{0:T(1024)}, u32[]{:S(2)}) copy-start(f32[16384]{0:T(1024)} %param.9) | copy-start | bytes 196612
  3.5 0.7 copy-start.5
  4.2 0.7 copy-start.7
  4.9 0.7 copy-start.9
  13.1 1.2 %copy-start.1 = (f32[12,16384]{1,0:T(8,128)S(1)}, f32[12,16384]{1,0:T(8,128)}, u32[]{:S(2)}) copy-start(f32[12,16384]{1,0:T(8,128)} %w_hbm.1) | copy-start | bytes 2359300
  14.3 0.8 %copy-start.2 = (f32[16384]{0:T(1024)S(1)}, f32[16384]{0:T(1024)}, u32[]{:S(2)}) copy-start(f32[16384]{0:T(1024)} %param.11) | copy-start | bytes 196612
  15.1 0.7 copy-start.6
  15.8 0.7 copy-start.8

commit v2 on v1

--- a/solution.py
+++ b/solution.py
@@ -70,7 +70,52 @@
     return first, second, along_y
 
 
-def spread_kernel(count, base, reach, w, direction, residual, grid, live_dir, live_res, live, table):
+def fetch(pairs, sem):
+    copies = [pltpu.make_async_copy(src, dst, sem.at[i]) for i, (src, dst) in enumerate(pairs)]
+    for copy in copies:
+        copy.start()
+    return copies
+
+
+def spread_kernel(
+    count_hbm,
+    base_hbm,
+    reach_hbm,
+    w_hbm,
+    direction_hbm,
+    residual_hbm,
+    grid,
+    live_dir,
+    live_res,
+    live,
+    table,
+    count,
+    base,
+    reach,
+    w,
+    direction,
+    residual,
+    sem,
+):
+    copies = fetch(
+        (
+            (reach_hbm, reach),
+            (w_hbm, w),
+            (count_hbm, count),
+            (base_hbm, base),
+            (direction_hbm, direction),
+            (residual_hbm, residual),
+        ),
+        sem,
+    )
+
+    def clear(x, carry):
+        for half in range(2):
+            grid[x, half] = jnp.zeros((ROWS, LANES), F32)
+        return carry
+
+    lax.fori_loop(0, WX, clear, 0)
+    copies[0].wait()
     anchor_x = lax.axis_index("gx") * NX
     anchor_y = lax.axis_index("gy") * NY
     anchor_z = lax.axis_index("gz") * NZ
@@ -87,13 +132,8 @@
         inside = (lane >= start) & (lane < start + COPIES)
         second = jnp.where(inside, outgoing(kind, source, NZ, length), second)
     table[1] = second * scale
-
-    def clear(x, carry):
-        for half in range(2):
-            grid[x, half] = jnp.zeros((ROWS, LANES), F32)
-        return carry
-
-    lax.fori_loop(0, WX, clear, 0)
+    for copy in copies[1:]:
+        copy.wait()
     low = iota((8, LANES), 0) < 4
     slot = iota((1, LANES), 1)
 
@@ -126,7 +166,7 @@
                 grid[spot] = grid[spot] + jnp.where(keep, parts[a // 2][half], 0.0)
         return carry
 
-    lax.fori_loop(0, TILES, tile, 0, unroll=2)
+    lax.fori_loop(0, TILES, tile, 0, unroll=8)
 
 
 def partner(axis, me, offset, count):
@@ -135,16 +175,19 @@
 
 def solve_kernel(
     sizes,
-    base,
-    reach,
+    base_hbm,
+    reach_hbm,
+    noise_hbm,
+    w_hbm,
     grid,
     live_dir,
     live_res,
     live,
-    noise,
-    w_hbm,
     image,
     sums,
+    base,
+    reach,
+    noise,
     w,
     forward,
     smooth,
@@ -169,7 +212,7 @@
     sum_in_x,
     sum_mid,
     sum_in_yz,
-    w_sem,
+    in_sem,
     z_sem,
     z_fix_sem,
     y_sem,
@@ -186,8 +229,6 @@
     n_yz = n_gy * n_gz
     px, py, pz = lax.axis_index("gx"), lax.axis_index("gy"), lax.axis_index("gz")
     pyz = py * n_gz + pz
-    length_x, length_y, length_z = reach[0] * float(NX), reach[1] * float(NY), reach[2] * float(NZ)
-
     def yz_partner(offset):
         other = lax.rem(pyz + offset, n_yz)
         return {"gy": other // n_gz, "gz": lax.rem(other, n_gz)}
@@ -198,8 +239,9 @@
     for k in range(1, n_yz):
         pl.semaphore_signal(barrier, inc=1, device_id=yz_partner(k), device_id_type=MESH)
 
-    w_copy = pltpu.make_async_copy(w_hbm, w, w_sem)
-    w_copy.start()
+    copies_in = fetch(((reach_hbm, reach), (base_hbm, base), (noise_hbm, noise), (w_hbm, w)), in_sem)
+    copies_in[0].wait()
+    length_x, length_y, length_z = reach[0] * float(NX), reach[1] * float(NY), reach[2] * float(NZ)
 
     def remote(src, dst, send, recv, device):
         return pltpu.make_async_remote_copy(
@@ -460,7 +502,8 @@
             smooth[x, half, 0:LIVE, :] += jnp.where(px > 0, x_fix_in[0, kind, half], 0.0)
         for kind, x in enumerate((WX - 1, WX - 2)):
             smooth[x, half, 0:LIVE, :] += jnp.where(px + 1 < n_gx, x_fix_in[1, kind, half], 0.0)
-    w_copy.wait()
+    for copy in copies_in[1:]:
+        copy.wait()
 
     def tile_spot(t):
         at = pl.ds(pl.multiple_of(t * LANES, LANES), LANES)
@@ -496,7 +539,7 @@
         sampled[pl.ds(t, 1), :] = gather(rows, (first, second), at, z0)
         return carry
 
-    lax.fori_loop(0, TILES, near, 0, unroll=2)
+    lax.fori_loop(0, TILES, near, 0, unroll=8)
 
     for c in range(YT):
         copy = remote(x_prefix.at[0], x_far.at[:, :, chunk(c), :], x2_send.at[0], x2_recv.at[c], {"gx": c})
@@ -518,7 +561,7 @@
         sampled[pl.ds(t, 1), :] += gather([rows], [weight], at, z0)
         return carry
 
-    lax.fori_loop(0, TILES, far, 0, unroll=2)
+    lax.fori_loop(0, TILES, far, 0, unroll=8)
 
     value = live[...] * (sampled[...] + noise[...] * live_dir[...])
     image[...] = value
@@ -568,7 +611,10 @@
             pl.when(px != q)(copy.wait_send)
 
 
-def update_kernel(sums, iterate, live, live_dir, live_res, image, new_iterate, new_residual, new_direction):
+def update_kernel(
+    iterate_hbm, sums, live, live_dir, live_res, image, new_iterate, new_residual, new_direction, iterate, sem
+):
+    copies = fetch(((iterate_hbm, iterate),), sem)
     def total(row):
         return jnp.sum(sums[row : row + 1, :], axis=1, keepdims=True)
 
@@ -576,6 +622,7 @@
     step = norm_old / curvature
     norm_new = norm_old + step * (step * square - 2.0 * cross)
     held = live_res[...] - step * image[...]
+    copies[0].wait()
     new_iterate[...] = live[...] * iterate[...] + step * live_dir[...]
     new_residual[...] = held
     new_direction[...] = held + norm_new / norm_old * live_dir[...]
@@ -586,7 +633,11 @@
     n_yz = n_gy * n_gz
     square = (TILES, LANES)
     in_vmem = pl.BlockSpec(memory_space=pltpu.VMEM)
-    in_smem = pl.BlockSpec(memory_space=pltpu.SMEM)
+    in_hbm = pl.BlockSpec(memory_space=pltpu.HBM)
+    dma = pltpu.SemaphoreType.DMA
+
+    def away(x):
+        return pltpu.with_memory_space_constraint(x, pltpu.HBM)
 
     def keep(x):
         return pltpu.with_memory_space_constraint(x, pltpu.VMEM)
@@ -594,20 +645,38 @@
     grid, live_dir, live_res, live = pl.pallas_call(
         spread_kernel,
         out_shape=[pltpu.VMEM((WX, 2, ROWS, LANES), F32)] + [pltpu.VMEM(square, F32)] * 3,
-        in_specs=[in_smem] * 3 + [in_vmem] * 3,
+        in_specs=[in_hbm] * 6,
         out_specs=[in_vmem] * 4,
-        scratch_shapes=[pltpu.VMEM((2, 136, LANES), F32)],
+        scratch_shapes=[
+            pltpu.VMEM((2, 136, LANES), F32),
+            pltpu.SMEM((TILES,), jnp.int32),
+            pltpu.SMEM((3, TILES), jnp.int32),
+            pltpu.SMEM((3,), F32),
+            pltpu.VMEM((12, TILES * LANES), F32),
+            pltpu.VMEM(square, F32),
+            pltpu.VMEM(square, F32),
+            dma((6,)),
+        ],
         compiler_params=pltpu.CompilerParams(vmem_limit_bytes=16 << 20),
         name="spread",
-    )(tile_counts, stencil_base, reach, interp_weights, direction.reshape(square), residual.reshape(square))
-
-    dma = pltpu.SemaphoreType.DMA
+    )(
+        away(tile_counts),
+        away(stencil_base),
+        away(reach),
+        away(interp_weights),
+        away(direction.reshape(square)),
+        away(residual.reshape(square)),
+    )
+
     image, sums = pl.pallas_call(
         functools.partial(solve_kernel, sizes),
         out_shape=[pltpu.VMEM(square, F32), pltpu.VMEM((8, LANES), F32)],
-        in_specs=[in_smem] * 2 + [in_vmem] * 5 + [pl.BlockSpec(memory_space=pl.ANY)],
+        in_specs=[in_hbm] * 4 + [in_vmem] * 4,
         out_specs=[in_vmem] * 2,
         scratch_shapes=[
+            pltpu.SMEM((3, TILES), jnp.int32),
+            pltpu.SMEM((3,), F32),
+            pltpu.VMEM(square, F32),
             pltpu.VMEM((12, TILES * LANES), F32),
             pltpu.VMEM((WX, 2, ROWS, LANES), F32),
             pltpu.VMEM((WX, 2, ROWS, LANES), F32),
@@ -632,7 +701,7 @@
             pltpu.VMEM((15, 8, LANES), F32),
             pltpu.VMEM((8, LANES), F32),
             pltpu.VMEM((15, 8, LANES), F32),
-            dma,
+            dma((4,)),
             dma((2, 3)),
             dma((2, 2)),
             dma((2, 3)),
@@ -650,23 +719,24 @@
         ),
         name="solve",
     )(
-        stencil_base,
-        reach,
+        away(stencil_base),
+        away(reach),
+        away(noise.reshape(square)),
+        away(interp_weights),
         keep(grid),
         keep(live_dir),
         keep(live_res),
         keep(live),
-        noise.reshape(square),
-        interp_weights,
     )
 
     outs = pl.pallas_call(
         update_kernel,
         out_shape=[jax.ShapeDtypeStruct(square, F32)] * 3,
-        in_specs=[in_vmem] * 6,
+        in_specs=[in_hbm] + [in_vmem] * 5,
         out_specs=[in_vmem] * 3,
+        scratch_shapes=[pltpu.VMEM(square, F32), dma((1,))],
         name="update",
-    )(keep(sums), iterate.reshape(square), keep(live), keep(live_dir), keep(live_res), keep(image))
+    )(away(iterate.reshape(square)), keep(sums), keep(live), keep(live_dir), keep(live_res), keep(image))
     return tuple(out.reshape(-1) for out in outs)
 
 

time: 80.7 us -> 62.9 us (0.78)
  Pallas kernels: 71.4 us -> 62.1 us
  local copies, waits for them, and re-layouts: 8.28 us -> 0 us
    unnamed x20 -> x0, local copies, waits for them, and re-layouts: 8.28 us -> none
    pallas_call x1, Pallas kernels: 62.2 us -> 56.8 us  [body(): pl.pallas_call(functools.partial(solve_kernel, sizes), out_shape=[pltpu.V...]
    pallas_call x1, Pallas kernels: 7.53 us -> 3.79 us  [body(): pl.pallas_call(spread_kernel, out_shape=[pltpu.VMEM((WX, 2, ROWS, LANES),...]
where the time goes in v2:
time: 62.9 us; the launch traced here: 62.7 us
  Pallas kernels  62.1 us (99%)
  between operations  0.65 us (1%)
    pallas_call x1, Pallas kernels, body(): pl.pallas_call(functools.partial(solve_kernel, sizes), out_shape=[pltpu.V...  56.8 us
    pallas_call x1, Pallas kernels, body(): pl.pallas_call(spread_kernel, out_shape=[pltpu.VMEM((WX, 2, ROWS, LANES),...  3.79 us
    pallas_call x1, Pallas kernels, body(): pl.pallas_call(update_kernel, out_shape=[jax.ShapeDtypeStruct(square, F32...  1.53 us

profile of v2, /device:TPU:1, one launch (start us, length us, event | category | flops | bytes accessed | tf_op | source)
XLA Modules:
  0.0 62.7 jit_solution(193956107796668806)
XLA Ops:
  0.6 3.8 %spread.1 = (f32[35,2,80,128]{3,2,1,0:T(8,128)S(1)}, f32[128,128]{1,0:T(8,128)S(1)}, f32[128,128]{1,0:T(8,128)S(1)}, f32[128,128]{1,0:T(8,128)S(1)}) custom-call(s32[128]{0:T(128)} %count_hbm.1, s32[3,128]{1,0:T(4,128)} %base_hbm.3, f32[3]{0:T(128)} %reach_hbm.3, f32[12,16384]{1,0:T(8,128)} %w_hbm.3, f32[128,128]{1,0:T(8,128)} %bitcast.9, f32[128,128]{1,0:T(8,128)} %bitcast.10), custom_call_target="tpu_custom_call" | custom-call | tf_op jit(solution)/shard_map/spread/pallas_call | solution.py:645
  4.4 56.8 %solve.1 = (f32[128,128]{1,0:T(8,128)S(1)}, f32[8,128]{1,0:T(8,128)S(1)}) custom-call(s32[3,128]{1,0:T(4,128)} %base_hbm.3, f32[3]{0:T(128)} %reach_hbm.3, f32[128,128]{1,0:T(8,128)} %bitcast.7, f32[12,16384]{1,0:T(8,128)} %w_hbm.3, f32[35,2,80,128]{3,2,1,0:T(8,128)S(1)} %get-tuple-element.12.grid, f32[128,128]{1,0:T(8,128)S(1)} %get-tuple-element.13.live_dir, ...), custom_call_target="tpu_custom_call" | custom-call | tf_op jit(solution)/shard_map/solve/pallas_call | solution.py:671
  61.2 1.5 %update.1 = (f32[128,128]{1,0:T(8,128)}, f32[128,128]{1,0:T(8,128)}, f32[128,128]{1,0:T(8,128)}) custom-call(f32[128,128]{1,0:T(8,128)} %bitcast.8, f32[8,128]{1,0:T(8,128)S(1)} %get-tuple-element.16.sums, f32[128,128]{1,0:T(8,128)S(1)} %get-tuple-element.15.live, f32[128,128]{1,0:T(8,128)S(1)} %get-tuple-element.13.live_dir, ...), custom_call_target="tpu_custom_call" | custom-call | tf_op jit(solution)/shard_map/update/pallas_call | solution.py:732

commit v3 on v2

v3 whole, which is shorter than its diff:
```python
import functools

import jax
import jax.numpy as jnp
from jax import lax
from jax.experimental import pallas as pl
from jax.experimental.pallas import tpu as pltpu
from jax.sharding import PartitionSpec as P

F32 = jnp.float32
BF16 = jnp.bfloat16
LANES = 128
TILES = 128
NX, NY, NZ = 32, 64, 128
WX = NX + 3
TOP = 4
ROWS = 80
LIVE = 72
YT = LIVE // 8
OWN, SPARE, CHANNELS, COPIES = 5, 8, 6, 20
STACKS = -(-WX * YT // COPIES)
PAIRS = STACKS // 2
XROWS = 40
SIDE, FIX = XROWS, XROWS + 8
YMSG = FIX + 2 * XROWS
PACK = SPARE + CHANNELS - OWN
OWNERS = ROWS // 8
MESH = pl.DeviceIdType.MESH


def iota(shape, dim):
    return lax.broadcasted_iota(jnp.int32, shape, dim)


def full(value):
    return jnp.full((1, LANES), value, F32)


def decay(distance, length):
    return jnp.exp(-distance.astype(F32) / length)


def outgoing(kind, source, size, length):
    one = decay(full(1), length) - jnp.exp(full(1.0) / length)
    two = decay(full(2), length) - jnp.exp(full(2.0) / length)
    one, two = one[:, :1], two[:, :1]
    zero = jnp.zeros(source.shape, F32)
    if kind == 0:
        return decay(size + 1 - source, length)
    if kind == 1:
        return jnp.where(source == size, one, jnp.where(source == size + 1, two, zero))
    if kind == 2:
        return jnp.where(source == size + 1, one, zero)
    if kind == 3:
        return decay(source + 1, length)
    if kind == 4:
        return jnp.where(source == -1, two, jnp.where(source == 0, one, zero))
    return jnp.where(source == -1, one, zero)


def incoming(kind, cell, size, length):
    if kind == 0:
        return decay(cell - 1, length)
    if kind == 3:
        return decay(size - 1 - cell, length)
    target = {1: -1, 2: 0, 4: size + 1, 5: size}[kind]
    return jnp.where(cell == target, 1.0, 0.0).astype(F32)


def lane_roles(lane):
    spare = lane >= SPARE
    place = jnp.maximum(lane - SPARE, 0)
    copy = place // CHANNELS
    return jnp.where(spare, place - copy * CHANNELS, -1), jnp.where(spare, copy, -1)


def tile_weights(w8, low):
    along_y = jnp.where(low, pltpu.roll(w8, 4, 0), w8)
    first = jnp.where(low, w8[0:1], w8[1:2]) * along_y
    second = jnp.where(low, w8[2:3], w8[3:4]) * along_y
    return first, second, along_y


def fetch(pairs, sem):
    copies = [pltpu.make_async_copy(src, dst, sem.at[i]) for i, (src, dst) in enumerate(pairs)]
    for copy in copies:
        copy.start()
    return copies


def spread_kernel(
    count_hbm,
    base_hbm,
    reach_hbm,
    w_hbm,
    direction_hbm,
    residual_hbm,
    grid,
    live_dir,
    live_res,
    live,
    table,
    count,
    base,
    reach,
    w,
    direction,
    residual,
    sem,
):
    copies = fetch(
        (
            (reach_hbm, reach),
            (w_hbm, w),
            (count_hbm, count),
            (base_hbm, base),
            (direction_hbm, direction),
            (residual_hbm, residual),
        ),
        sem,
    )

    def clear(x, carry):
        for half in range(2):
            grid[x, half] = jnp.zeros((ROWS, LANES), F32)
        return carry

    lax.fori_loop(0, WX, clear, 0)
    copies[0].wait()
    anchor_x = lax.axis_index("gx") * NX
    anchor_y = lax.axis_index("gy") * NY
    anchor_z = lax.axis_index("gz") * NZ
    length = reach[2] * float(NZ)
    scale = 1.0 / (
        jnp.sqrt(full(reach[0] * float(NX))) * jnp.sqrt(full(reach[1] * float(NY))) * jnp.sqrt(full(length))
    )
    source = iota((136, LANES), 0) - 1
    lane = iota((136, LANES), 1)
    table[0] = decay(jnp.abs(lane - 1 - source), length) * scale
    own = (lane >= OWN) & (lane < SPARE)
    second = jnp.where(own, decay(jnp.abs(lane - OWN + NZ - 1 - source), length), 0.0)
    channel, _ = lane_roles(lane)
    for kind in range(CHANNELS):
        second = jnp.where(channel == kind, outgoing(kind, source, NZ, length), second)
    table[1] = second * scale
    for copy in copies[1:]:
        copy.wait()
    low = iota((8, LANES), 0) < 4
    slot = iota((1, LANES), 1)

    def tile(t, carry):
        at = pl.ds(pl.multiple_of(t * LANES, LANES), LANES)
        w8 = w[0:8, at]
        mask = slot < count[t]
        values = jnp.where(mask, direction[pl.ds(t, 1), :], 0.0)
        live_dir[pl.ds(t, 1), :] = values
        live_res[pl.ds(t, 1), :] = jnp.where(mask, residual[pl.ds(t, 1), :], 0.0)
        live[pl.ds(t, 1), :] = jnp.where(mask, 1.0, 0.0)
        first, second, _ = tile_weights(w8, low)
        x0 = base[0, t] - anchor_x + 1
        y0 = base[1, t] - anchor_y + 1 + TOP
        z0 = base[2, t] - anchor_z + 1
        parts = [[None, None], [None, None]]
        for e in range(4):
            along_z = w[8 + e : 9 + e, at] * values
            row = [table[half, pl.ds(z0 + e, 1), :] for half in range(2)]
            for pair, product in enumerate((first, second)):
                taps = jnp.sum(product * along_z, axis=1, keepdims=True)
                for half in range(2):
                    term = taps * row[half]
                    parts[pair][half] = term if e == 0 else parts[pair][half] + term
        for a in range(4):
            start = y0 if a % 2 == 0 else y0 - 4
            keep = low if a % 2 == 0 else jnp.logical_not(low)
            for half in range(2):
                spot = (x0 + a, half, pl.ds(start, 8), slice(None))
                grid[spot] = grid[spot] + jnp.where(keep, parts[a // 2][half], 0.0)
        return carry

    lax.fori_loop(0, TILES, tile, 0, unroll=16)


def solve_kernel(
    sizes,
    base_hbm,
    reach_hbm,
    noise_hbm,
    w_hbm,
    grid,
    live_dir,
    live_res,
    live,
    image,
    sums,
    base,
    reach,
    noise,
    w,
    smooth,
    basis,
    pick_z,
    pick_x,
    pick_y,
    x_side,
    x_out,
    x_in,
    x_prefix,
    x_far,
    x_fix_in,
    y_msg,
    y_side,
    diagonal,
    z_out,
    z_in,
    y_in,
    y_fix_in,
    diagonal_in,
    z_mixed,
    y_mixed,
    far,
    far_z,
    far_y,
    far_z_in,
    far_y_in,
    sampled,
    sum_out,
    sum_in_x,
    sum_mid,
    sum_in_yz,
    in_sem,
    x_sem,
    x_back_sem,
    x_fix_sem,
    z_sem,
    y_sem,
    y_fix_sem,
    d_sem,
    fz_sem,
    fy_sem,
    sx_sem,
    syz_sem,
):
    n_gx, n_gy, n_gz = sizes
    n_yz = n_gy * n_gz
    px, py, pz = lax.axis_index("gx"), lax.axis_index("gy"), lax.axis_index("gz")
    pyz = py * n_gz + pz

    def at_x(k):
        return {"gx": lax.rem(px + k, n_gx)}

    def at_yz(ky, kz):
        return {"gy": lax.rem(py + ky, n_gy), "gz": lax.rem(pz + kz, n_gz)}

    def around_yz(k):
        other = lax.rem(pyz + k, n_yz)
        return {"gy": other // n_gz, "gz": lax.rem(other, n_gz)}

    barrier = pltpu.get_barrier_semaphore()
    for k in range(1, n_gx):
        pl.semaphore_signal(barrier, inc=1, device_id=at_x(k), device_id_type=MESH)
    for k in range(1, n_yz):
        pl.semaphore_signal(barrier, inc=1, device_id=around_yz(k), device_id_type=MESH)
    copies_in = fetch(((reach_hbm, reach), (base_hbm, base), (noise_hbm, noise), (w_hbm, w)), in_sem)
    copies_in[0].wait()
    length_x, length_y, length_z = reach[0] * float(NX), reach[1] * float(NY), reach[2] * float(NZ)
    sent = []

    def chunk(c):
        return pl.ds(pl.multiple_of(c * 8, 8), 8)

    def send(src, dst, sems, index, device, when=None, slot=None):
        copy = pltpu.make_async_remote_copy(
            src_ref=src,
            dst_ref=dst,
            send_sem=sems.at[0, index],
            recv_sem=sems.at[1, index if slot is None else slot],
            device_id=device,
            device_id_type=MESH,
        )
        if when is None:
            copy.start()
            sent.append(copy.wait_send)
        else:
            pl.when(when)(copy.start)
            sent.append(lambda: pl.when(when)(copy.wait_send))
        return copy

    def way(pos, k, count):
        return jnp.where(pos + k < count, 0, 1)

    def mix(pos, count, size, length, k):
        from_left = pos >= k
        left = jnp.where(from_left, jnp.exp(full(-float(size * (k - 1))) / length), 0.0)
        right = jnp.where(from_left, 0.0, jnp.exp(full(-float(size * (count - k - 1))) / length))
        next_left = jnp.where(from_left, full(1.0), 0.0) if k == 1 else full(0.0)
        next_right = jnp.where(from_left, 0.0, full(1.0)) if count - k == 1 else full(0.0)
        return (left, next_left), (right, next_right)

    sub = iota((8, LANES), 0)
    lane = iota((8, LANES), 1)
    low = sub < 4
    channel, copy_of = lane_roles(lane)
    first_kinds = (channel >= 0) & (channel < 3)
    is_moment = (channel == 0) | (channel == 3)

    step_x = jnp.exp(full(-1.0) / length_x)
    fix_one = step_x - jnp.exp(full(1.0) / length_x)
    fix_two = jnp.exp(full(-2.0) / length_x) - jnp.exp(full(2.0) / length_x)

    def scan(yt, carry):
        rows = pl.ds(pl.multiple_of(yt * 8, 8), 8)
        for half, out in enumerate((x_out, x_side)):
            state = grid[0, half, rows, :]
            smooth[0, half, rows, :] = state
            for x in range(1, WX):
                state = grid[x, half, rows, :] + step_x * state
                smooth[x, half, rows, :] = state
            out[0, rows, :] = state
            edge = [grid[x, half, rows, :] for x in (0, 1, WX - 2, WX - 1)]
            out[2, rows, :] = edge[2] * fix_one + edge[3] * fix_two
            out[3, rows, :] = edge[3] * fix_one
            out[4, rows, :] = edge[0] * fix_two + edge[1] * fix_one
            out[5, rows, :] = edge[0] * fix_one
            state = step_x * edge[3]
            for x in reversed(range(WX - 1)):
                smooth[x, half, rows, :] = smooth[x, half, rows, :] + state
                if x == 0:
                    out[1, rows, :] = state + edge[0]
                else:
                    state = step_x * (state + grid[x, half, rows, :])
        return carry

    lax.fori_loop(0, YT, scan, 0)
    for x in range(WX):
        for half in range(2):
            smooth[x, half, LIVE:ROWS, :] = jnp.zeros((ROWS - LIVE, LANES), F32)
    for plane in range(6):
        total = jnp.zeros((8, LANES), F32)
        for yt in range(YT):
            moved = pltpu.roll(x_side[plane, 8 * yt : 8 * yt + 8, :], (PACK * yt - OWN) % LANES, 1)
            total = jnp.where((lane >= PACK * yt) & (lane < PACK * (yt + 1)), moved, total)
        x_out[plane, LIVE:ROWS, :] = total

    def unpack(packed, yt):
        place = PACK * yt + jnp.where(lane < SPARE, jnp.maximum(lane - OWN, 0), channel + SPARE - OWN)
        return jnp.where(lane < OWN, 0.0, jnp.take_along_axis(packed, place, axis=1))

    pl.semaphore_wait(barrier, n_gx - 1 + n_yz - 1)
    x_right = send(x_out.at[pl.ds(2, 2)], x_fix_in.at[0], x_fix_sem, 0, at_x(1), px + 1 < n_gx)
    x_left = send(x_out.at[pl.ds(4, 2)], x_fix_in.at[1], x_fix_sem, 1, at_x(n_gx - 1), px > 0)
    for c in range(OWNERS):
        send(x_out.at[pl.ds(0, 2), chunk(c), :], x_in.at[px], x_sem, c, {"gx": c}, px != c, px)

    row = iota((96, 3 * ROWS), 0)
    col = iota((96, 3 * ROWS), 1)
    part = col // ROWS
    source = col - part * ROWS - TOP - 1
    cell = row - TOP - 1
    entry = jnp.where((cell >= -1) & (cell <= NY + 1), decay(jnp.abs(cell - source), length_y), 0.0)
    for kind in range(CHANNELS):
        entry = jnp.where(row == ROWS + kind + kind // 3, outgoing(kind, source, NY, length_y), entry)
    entry = jnp.where((source >= -1) & (source <= NY + 1), entry, 0.0)
    entry_high = entry.astype(BF16).astype(F32)
    basis[...] = jnp.where(part == 1, entry - entry_high, entry_high).astype(BF16)

    def contract(planes):
        values = jnp.concatenate(planes, axis=1)
        high = values.astype(BF16)
        rest = (values - high.astype(F32)).astype(BF16)
        stacked = jnp.concatenate([high, high, rest], axis=0)
        return jnp.dot(basis[...], stacked, preferred_element_type=F32)

    def back(q):
        return pltpu.make_async_remote_copy(
            src_ref=x_prefix.at[q],
            dst_ref=x_far.at[:, chunk(px), :],
            send_sem=x_back_sem.at[0, q],
            recv_sem=x_back_sem.at[1, px],
            device_id={"gx": q},
            device_id_type=MESH,
        )

    def contract_own(x):
        result = contract([smooth[x, 0], smooth[x, 1]])
        for half in range(2):
            smooth[x, half] = result[:ROWS, LANES * half : LANES * (half + 1)]
        for side in range(2):
            for kind in range(3):
                line = result[ROWS + 4 * side + kind : ROWS + 4 * side + kind + 1]
                start = 0 if kind == 0 else FIX + XROWS * (kind - 1)
                y_msg[side, pl.ds(start + x, 1), :] = line[:, :LANES]
                y_side[side, kind, pl.ds(x, 1), :] = line[:, LANES:]

    def contract_step(x, carry):
        contract_own(x)
        return carry

    lax.fori_loop(2, WX - 3, contract_step, 0, unroll=5)

    def received(dst, sems, slot):
        pltpu.make_async_remote_copy(
            src_ref=dst,
            dst_ref=dst,
            send_sem=sems.at[0, slot],
            recv_sem=sems.at[1, slot],
            device_id={"gx": slot},
            device_id_type=MESH,
        ).wait_recv()

    ratio = jnp.exp(full(-float(NX)) / length_x)

    @pl.when(px < OWNERS)
    def _():
        x_in[px] = x_out[0:2, chunk(px), :]
        for p in range(n_gx):
            pl.when(px != p)(lambda: received(x_in.at[p], x_sem, p))
        for side, order in enumerate((range(n_gx), reversed(range(n_gx)))):
            total = jnp.zeros((8, LANES), F32)
            for q in order:
                x_prefix[q, side] = total
                total = total * ratio + x_in[q, side]
        x_far[:, chunk(px), :] = x_prefix[px]
        for q in range(n_gx):
            pl.when(px != q)(back(q).start)

    if n_gx > 1:
        pl.when(px > 0)(x_right.wait_recv)
        pl.when(px + 1 < n_gx)(x_left.wait_recv)
    for side, valid, places in ((0, px > 0, (0, 1)), (1, px + 1 < n_gx, (WX - 1, WX - 2))):
        for kind, x in enumerate(places):
            smooth[x, 0, 0:LIVE, :] += jnp.where(valid, x_fix_in[side, kind, 0:LIVE, :], 0.0)
            packed = jnp.where(valid, x_fix_in[side, kind, LIVE:ROWS, :], 0.0)
            for yt in range(YT):
                smooth[x, 1, 8 * yt : 8 * yt + 8, :] += unpack(packed, yt)
    for x in (0, 1, WX - 3, WX - 2, WX - 1):
        contract_own(x)

    stacks = [jnp.zeros((8, LANES), F32) for _ in range(STACKS)]
    for j in range(WX * YT):
        x, yt = divmod(j, YT)
        stack, copy = divmod(j, COPIES)
        stacks[stack] = jnp.where(copy_of == copy, smooth[x, 1, 8 * yt : 8 * yt + 8, :], stacks[stack])
    for pair in range(PAIRS):
        one, two = stacks[2 * pair], stacks[2 * pair + 1]
        z_out[0, pair] = jnp.where(first_kinds, one, pltpu.roll(two, 3, 1))
        z_out[1, pair] = jnp.where(first_kinds, pltpu.roll(one, LANES - 3, 1), two)
    for side in range(2):
        beside = jnp.zeros((8, LANES), F32)
        both = jnp.zeros((8, LANES), F32)
        for j in range(15):
            kind, xt = divmod(j, 5)
            value = y_side[side, kind, 8 * xt : 8 * xt + 8, :]
            moved = pltpu.roll(value, 8 * j, 1) if j else value
            beside = jnp.where((lane >= 8 * j) & (lane < 8 * j + 8), moved, beside)
            both = jnp.where(copy_of == j, value, both)
        y_msg[side, SIDE : SIDE + 8, :] = beside
        diagonal[side] = both
    z_copies = [
        send(z_out.at[way(pz, k, n_gz)], z_in.at[k - 1], z_sem, k - 1, at_yz(0, k)) for k in range(1, n_gz)
    ]
    y_copies = [
        send(y_msg.at[way(py, k, n_gy), pl.ds(0, FIX), :], y_in.at[k - 1], y_sem, k - 1, at_yz(k, 0))
        for k in range(1, n_gy)
    ]
    y_right = y_left = None
    if n_gy > 1:
        fixes = pl.ds(FIX, 2 * XROWS)
        y_right = send(y_msg.at[0, fixes, :], y_fix_in.at[0], y_fix_sem, 0, at_yz(1, 0), py + 1 < n_gy)
        y_left = send(y_msg.at[1, fixes, :], y_fix_in.at[1], y_fix_sem, 1, at_yz(n_gy - 1, 0), py > 0)
    d_copies = {}
    for ky in range(1, n_gy):
        for kz in range(1, n_gz):
            index = (ky - 1) * (n_gz - 1) + kz - 1
            d_copies[ky, kz] = send(
                diagonal.at[way(py, ky, n_gy)], diagonal_in.at[index], d_sem, index, at_yz(ky, kz)
            )

    cell = iota((136, LANES), 0) - 1
    wide = iota((136, LANES), 1)
    pick_z[0] = jnp.where(wide == cell + 1, 1.0, 0.0).astype(F32)
    picked = jnp.where((wide >= OWN) & (wide < SPARE) & (wide - OWN + NZ - 1 == cell), 1.0, 0.0).astype(F32)
    wide_channel, _ = lane_roles(wide)
    for kind in range(CHANNELS):
        picked = jnp.where(wide_channel == kind, incoming(kind, cell, NZ, length_z), picked)
    pick_z[1] = picked
    cell = iota((XROWS, LANES), 0) - 1
    for side in range(2):
        pick_x[side] = incoming(3 * side, cell, NX, length_x)
    cell = iota((ROWS, LANES), 0) - TOP - 1
    for side in range(2):
        pick_y[side] = incoming(3 * side, cell, NY, length_y)

    for c in range(OWNERS):
        pl.when(px != c)(lambda: received(x_far.at[:, chunk(c), :], x_back_sem, c))
    for side in range(2):
        far[side, 0, 0:LIVE, :] = x_far[side, 0:LIVE, :]
        for yt in range(YT):
            far[side, 1, 8 * yt : 8 * yt + 8, :] = unpack(x_far[side, LIVE:ROWS, :], yt)
        for half in range(2):
            far[side, half, LIVE:ROWS, :] = jnp.zeros((ROWS - LIVE, LANES), F32)
    total = jnp.zeros((8, LANES), F32)
    for side in range(2):
        result = contract([far[side, 0], far[side, 1]])
        for half in range(2):
            values = result[:, LANES * half : LANES * (half + 1)]
            far[side, half] = values[:ROWS]
            for to in range(2):
                far_y[to, half, 4 * side : 4 * side + 4, :] = values[ROWS + 4 * to : ROWS + 4 * to + 4]
        for yt in range(YT):
            j = side * YT + yt
            total = jnp.where(copy_of == j, result[8 * yt : 8 * yt + 8, LANES:], total)
    far_z[...] = total
    far_z_copies = [send(far_z, far_z_in.at[k - 1], fz_sem, k - 1, at_yz(0, k)) for k in range(1, n_gz)]
    far_y_copies = {}
    for ky in range(1, n_gy):
        for kz in range(n_gz):
            index = (ky - 1) * n_gz + kz
            far_y_copies[ky, kz] = send(
                far_y.at[way(py, ky, n_gy)], far_y_in.at[index], fy_sem, index, at_yz(ky, kz)
            )

    def channel_weights(k):
        (left, next_left), (right, next_right) = mix(pz, n_gz, NZ, length_z, k)
        return jnp.where(
            first_kinds,
            jnp.where(is_moment, left, next_left),
            jnp.where(channel >= 3, jnp.where(is_moment, right, next_right), 0.0),
        )

    from_z = [[jnp.zeros((8, LANES), F32) for _ in range(PAIRS)] for _ in range(2)]
    for k in range(1, n_gz):
        z_copies[k - 1].wait_recv()
        weights = [jnp.where(is_moment, moment, fix) for moment, fix in mix(pz, n_gz, NZ, length_z, k)]
        for pair in range(PAIRS):
            got = z_in[k - 1, pair]
            for side in range(2):
                from_z[side][pair] = from_z[side][pair] + weights[side] * got
    for pair in range(PAIRS):
        one, two = from_z[0][pair], from_z[1][pair]
        z_mixed[2 * pair] = jnp.where(first_kinds, one, pltpu.roll(two, 3, 1))
        z_mixed[2 * pair + 1] = jnp.where(first_kinds, pltpu.roll(one, LANES - 3, 1), two)
    beside = [jnp.zeros((8, LANES), F32) for _ in range(2)]
    both = [jnp.zeros((8, LANES), F32) for _ in range(2)]
    lines = [[jnp.zeros((8, LANES), F32) for _ in range(XROWS // 8)] for _ in range(2)]
    for ky in range(1, n_gy):
        y_copies[ky - 1].wait_recv()
        weights = mix(py, n_gy, NY, length_y, ky)
        for side in range(2):
            moment, fix = weights[side]
            for tile in range(XROWS // 8):
                lines[side][tile] = lines[side][tile] + moment * y_in[ky - 1, 8 * tile : 8 * tile + 8, :]
            beside[side] = beside[side] + jnp.where(lane < 40, moment, fix) * y_in[ky - 1, SIDE : SIDE + 8, :]
        for kz in range(1, n_gz):
            d_copies[ky, kz].wait_recv()
            got = channel_weights(kz) * diagonal_in[(ky - 1) * (n_gz - 1) + kz - 1]
            for side in range(2):
                moment, fix = weights[side]
                both[side] = both[side] + jnp.where(copy_of < 5, moment, fix) * got
    if n_gy > 1:
        pl.when(py > 0)(y_right.wait_recv)
        pl.when(py + 1 < n_gy)(y_left.wait_recv)
    for side, valid in enumerate((py > 0, py + 1 < n_gy)):
        for tile in range(XROWS // 8):
            y_mixed[side, 0, 0, 8 * tile : 8 * tile + 8, :] = lines[side][tile]
        for kind in range(1, 3):
            start = XROWS * (kind - 1)
            y_mixed[side, kind, 0] = jnp.where(valid, y_fix_in[side, start : start + XROWS, :], 0.0)
        for j in range(15):
            kind, xt = divmod(j, 5)
            moved = pltpu.roll(beside[side], LANES - 8 * j, 1) if j else beside[side]
            y_mixed[side, kind, 1, 8 * xt : 8 * xt + 8, :] = jnp.where(
                lane < SPARE, moved, jnp.where(copy_of == j, both[side], 0.0)
            )

    def expand(x, carry):
        for half in range(2):
            line = [
                [y_mixed[side, kind, half, pl.ds(x, 1), :] for kind in range(3)] for side in range(2)
            ]
            for yt in range(YT):
                rows = slice(8 * yt, 8 * yt + 8)
                value = smooth[x, half, rows, :]
                if half == 1:
                    j = x * YT + yt
                    stack = j // COPIES
                    value = jnp.where(
                        lane < SPARE, value, jnp.where(copy_of == j - stack * COPIES, z_mixed[stack], 0.0)
                    )
                for side in range(2):
                    value = value + pick_y[side, rows, :] * line[side][0]
                if yt == 0:
                    value = value + jnp.where(sub == 4, line[0][1], jnp.where(sub == 5, line[0][2], 0.0))
                if yt == YT - 1:
                    value = value + jnp.where(sub == 6, line[1][1], jnp.where(sub == 5, line[1][2], 0.0))
                smooth[x, half, rows, :] = value
        return carry

    lax.fori_loop(0, WX, expand, 0)
    for copy in copies_in[1:]:
        copy.wait()

    def tile_spot(t):
        at = pl.ds(pl.multiple_of(t * LANES, LANES), LANES)
        x0 = jnp.clip(base[0, t] - px * NX + 1, 0, NX - 1)
        y0 = jnp.clip(base[1, t] - py * NY + 1, 0, NY - 1) + TOP
        z0 = jnp.clip(base[2, t] - pz * NZ + 1, 0, NZ - 1)
        return at, x0, y0, z0

    def gather(rows, weights, at, z0):
        total = None
        for e in range(4):
            pick = [pick_z[half, pl.ds(z0 + e, 1), :] for half in range(2)]
            inner = None
            for cells, weight in zip(rows, weights):
                taps = jnp.sum(cells[0] * pick[0] + cells[1] * pick[1], axis=1, keepdims=True)
                inner = weight * taps if inner is None else inner + weight * taps
            inner = inner * w[8 + e : 9 + e, at]
            total = inner if e == 0 else total + inner
        return jnp.sum(total, axis=0, keepdims=True)

    def near(t, carry):
        at, x0, y0, z0 = tile_spot(t)
        first, second, _ = tile_weights(w[0:8, at], low)
        rows = [
            [
                jnp.where(
                    low, smooth[x0 + a, half, pl.ds(y0, 8), :], smooth[x0 + a + 1, half, pl.ds(y0 - 4, 8), :]
                )
                for half in range(2)
            ]
            for a in (0, 2)
        ]
        sampled[pl.ds(t, 1), :] = gather(rows, (first, second), at, z0)
        return carry

    lax.fori_loop(0, TILES, near, 0, unroll=16)

    from_z = jnp.zeros((8, LANES), F32)
    for k in range(1, n_gz):
        far_z_copies[k - 1].wait_recv()
        from_z = from_z + channel_weights(k) * far_z_in[k - 1]
    lines = [[jnp.zeros((8, LANES), F32) for _ in range(2)] for _ in range(2)]
    for ky in range(1, n_gy):
        weights = mix(py, n_gy, NY, length_y, ky)
        weights = [jnp.where((sub == 0) | (sub == 4), moment, fix) for moment, fix in weights]
        for kz in range(n_gz):
            far_y_copies[ky, kz].wait_recv()
            index = (ky - 1) * n_gz + kz
            got = [far_y_in[index, half] for half in range(2)]
            if kz == 0:
                got[1] = jnp.where(lane < SPARE, got[1], 0.0)
            else:
                got = [None, jnp.where(copy_of == 0, channel_weights(kz) * got[1], 0.0)]
            for side in range(2):
                for half in range(2):
                    if got[half] is not None:
                        lines[side][half] = lines[side][half] + weights[side] * got[half]
    for x in range(2):
        for half in range(2):
            line = [[lines[side][half][4 * x + kind : 4 * x + kind + 1] for kind in range(3)] for side in range(2)]
            for yt in range(YT):
                rows = slice(8 * yt, 8 * yt + 8)
                value = far[x, half, rows, :]
                if half == 1:
                    value = jnp.where(lane < SPARE, value, jnp.where(copy_of == x * YT + yt, from_z, 0.0))
                for side in range(2):
                    value = value + pick_y[side, rows, :] * line[side][0]
                if yt == 0:
                    value = value + jnp.where(sub == 4, line[0][1], jnp.where(sub == 5, line[0][2], 0.0))
                if yt == YT - 1:
                    value = value + jnp.where(sub == 6, line[1][1], jnp.where(sub == 5, line[1][2], 0.0))
                far[x, half, rows, :] = value

    def distant(t, carry):
        at, x0, y0, z0 = tile_spot(t)
        w8 = w[0:8, at]
        _, _, along_y = tile_weights(w8, low)
        along_x = []
        for side in range(2):
            total = None
            for a in range(4):
                term = w8[a : a + 1] * pick_x[side, pl.ds(x0 + a, 1), :]
                total = term if a == 0 else total + term
            along_x.append(total)
        weight = jnp.where(low, along_x[0], along_x[1]) * along_y
        rows = [jnp.where(low, far[0, half, pl.ds(y0, 8), :], far[1, half, pl.ds(y0 - 4, 8), :]) for half in range(2)]
        sampled[pl.ds(t, 1), :] += gather([rows], [weight], at, z0)
        return carry

    lax.fori_loop(0, TILES, distant, 0, unroll=16)

    value = live[...] * (sampled[...] + noise[...] * live_dir[...])
    image[...] = value
    pairs = (
        (live_res[...], live_res[...]),
        (live_dir[...], value),
        (live_res[...], value),
        (value, value),
    )
    sum_out[...] = jnp.concatenate(
        [jnp.sum(a * b, axis=0, keepdims=True) for a, b in pairs] + [jnp.zeros((4, LANES), F32)], axis=0
    )
    copies = [send(sum_out, sum_in_x.at[k - 1], sx_sem, k - 1, at_x(k)) for k in range(1, n_gx)]
    total = sum_out[...]
    for k in range(1, n_gx):
        copies[k - 1].wait_recv()
        total = total + sum_in_x[k - 1]
    sum_mid[...] = total
    copies = [send(sum_mid, sum_in_yz.at[k - 1], syz_sem, k - 1, around_yz(k)) for k in range(1, n_yz)]
    for k in range(1, n_yz):
        copies[k - 1].wait_recv()
        total = total + sum_in_yz[k - 1]
    sums[...] = total
    for wait in sent:
        wait()

    @pl.when(px < OWNERS)
    def _():
        for q in range(n_gx):
            pl.when(px != q)(back(q).wait_send)


def update_kernel(
    iterate_hbm, sums, live, live_dir, live_res, image, new_iterate, new_residual, new_direction, iterate, sem
):
    copies = fetch(((iterate_hbm, iterate),), sem)
    def total(row):
        return jnp.sum(sums[row : row + 1, :], axis=1, keepdims=True)

    norm_old, curvature, cross, square = total(0), total(1), total(2), total(3)
    step = norm_old / curvature
    norm_new = norm_old + step * (step * square - 2.0 * cross)
    held = live_res[...] - step * image[...]
    copies[0].wait()
    new_iterate[...] = live[...] * iterate[...] + step * live_dir[...]
    new_residual[...] = held
    new_direction[...] = held + norm_new / norm_old * live_dir[...]


def body(sizes, iterate, residual, direction, noise, stencil_base, interp_weights, tile_counts, reach):
    n_gx, n_gy, n_gz = sizes
    n_yz = n_gy * n_gz
    square = (TILES, LANES)
    in_vmem = pl.BlockSpec(memory_space=pltpu.VMEM)
    in_hbm = pl.BlockSpec(memory_space=pltpu.HBM)
    dma = pltpu.SemaphoreType.DMA

    def away(x):
        return pltpu.with_memory_space_constraint(x, pltpu.HBM)

    def keep(x):
        return pltpu.with_memory_space_constraint(x, pltpu.VMEM)

    grid, live_dir, live_res, live = pl.pallas_call(
        spread_kernel,
        out_shape=[pltpu.VMEM((WX, 2, ROWS, LANES), F32)] + [pltpu.VMEM(square, F32)] * 3,
        in_specs=[in_hbm] * 6,
        out_specs=[in_vmem] * 4,
        scratch_shapes=[
            pltpu.VMEM((2, 136, LANES), F32),
            pltpu.SMEM((TILES,), jnp.int32),
            pltpu.SMEM((3, TILES), jnp.int32),
            pltpu.SMEM((3,), F32),
            pltpu.VMEM((12, TILES * LANES), F32),
            pltpu.VMEM(square, F32),
            pltpu.VMEM(square, F32),
            dma((6,)),
        ],
        compiler_params=pltpu.CompilerParams(vmem_limit_bytes=16 << 20),
        name="spread",
    )(
        away(tile_counts),
        away(stencil_base),
        away(reach),
        away(interp_weights),
        away(direction.reshape(square)),
        away(residual.reshape(square)),
    )

    image, sums = pl.pallas_call(
        functools.partial(solve_kernel, sizes),
        out_shape=[pltpu.VMEM(square, F32), pltpu.VMEM((8, LANES), F32)],
        in_specs=[in_hbm] * 4 + [in_vmem] * 4,
        out_specs=[in_vmem] * 2,
        scratch_shapes=[
            pltpu.SMEM((3, TILES), jnp.int32),
            pltpu.SMEM((3,), F32),
            pltpu.VMEM(square, F32),
            pltpu.VMEM((12, TILES * LANES), F32),
            pltpu.VMEM((WX, 2, ROWS, LANES), F32),
            pltpu.VMEM((96, 3 * ROWS), BF16),
            pltpu.VMEM((2, 136, LANES), F32),
            pltpu.VMEM((2, XROWS, LANES), F32),
            pltpu.VMEM((2, ROWS, LANES), F32),
            pltpu.VMEM((6, LIVE, LANES), F32),
            pltpu.VMEM((6, ROWS, LANES), F32),
            pltpu.VMEM((n_gx, 2, 8, LANES), F32),
            pltpu.VMEM((n_gx, 2, 8, LANES), F32),
            pltpu.VMEM((2, ROWS, LANES), F32),
            pltpu.VMEM((2, 2, ROWS, LANES), F32),
            pltpu.VMEM((2, YMSG, LANES), F32),
            pltpu.VMEM((2, 3, XROWS, LANES), F32),
            pltpu.VMEM((2, 8, LANES), F32),
            pltpu.VMEM((2, PAIRS, 8, LANES), F32),
            pltpu.VMEM((3, PAIRS, 8, LANES), F32),
            pltpu.VMEM((3, FIX, LANES), F32),
            pltpu.VMEM((2, 2 * XROWS, LANES), F32),
            pltpu.VMEM((9, 8, LANES), F32),
            pltpu.VMEM((STACKS, 8, LANES), F32),
            pltpu.VMEM((2, 3, 2, XROWS, LANES), F32),
            pltpu.VMEM((2, 2, ROWS, LANES), F32),
            pltpu.VMEM((8, LANES), F32),
            pltpu.VMEM((2, 2, 8, LANES), F32),
            pltpu.VMEM((3, 8, LANES), F32),
            pltpu.VMEM((12, 2, 8, LANES), F32),
            pltpu.VMEM(square, F32),
            pltpu.VMEM((8, LANES), F32),
            pltpu.VMEM((15, 8, LANES), F32),
            pltpu.VMEM((8, LANES), F32),
            pltpu.VMEM((15, 8, LANES), F32),
            dma((4,)),
            dma((2, n_gx)),
            dma((2, n_gx)),
            dma((2, 2)),
            dma((2, 3)),
            dma((2, 3)),
            dma((2, 2)),
            dma((2, 9)),
            dma((2, 3)),
            dma((2, 12)),
            dma((2, 15)),
            dma((2, 15)),
        ],
        compiler_params=pltpu.CompilerParams(
            collective_id=0, has_side_effects=True, vmem_limit_bytes=24 << 20
        ),
        name="solve",
    )(
        away(stencil_base),
        away(reach),
        away(noise.reshape(square)),
        away(interp_weights),
        keep(grid),
        keep(live_dir),
        keep(live_res),
        keep(live),
    )

    outs = pl.pallas_call(
        update_kernel,
        out_shape=[jax.ShapeDtypeStruct(square, F32)] * 3,
        in_specs=[in_hbm] + [in_vmem] * 5,
        out_specs=[in_vmem] * 3,
        scratch_shapes=[pltpu.VMEM(square, F32), dma((1,))],
        name="update",
    )(away(iterate.reshape(square)), keep(sums), keep(live), keep(live_dir), keep(live_res), keep(image))
    return tuple(out.reshape(-1) for out in outs)


def solution(mesh):
    sizes = tuple(mesh.shape[axis] for axis in ("gx", "gy", "gz"))
    lines = P(("gx", "gy", "gz"))
    return jax.shard_map(
        functools.partial(body, sizes),
        mesh=mesh,
        in_specs=(lines, lines, lines, lines, P(None, ("gx", "gy", "gz")), P(None, ("gx", "gy", "gz")), lines, P()),
        out_specs=(lines, lines, lines),
        check_vma=False,
    )
```

time: 62.9 us -> 48.2 us (0.77)
  Pallas kernels: 62.1 us -> 47.4 us
    pallas_call x1, Pallas kernels: 56.8 us -> 42.7 us  [body(): pl.pallas_call(functools.partial(solve_kernel, sizes), out_shape=[pltpu.V...]
    pallas_call x1, Pallas kernels: 3.79 us -> 3.11 us  [body(): pl.pallas_call(spread_kernel, out_shape=[pltpu.VMEM((WX, 2, ROWS, LANES),...]
where the time goes in v3:
time: 48.2 us; the launch traced here: 48 us
  Pallas kernels  47.4 us (98%)
  between operations  0.65 us (1%)
    pallas_call x1, Pallas kernels, body(): pl.pallas_call(functools.partial(solve_kernel, sizes), out_shape=[pltpu.V...  42.7 us
    pallas_call x1, Pallas kernels, body(): pl.pallas_call(spread_kernel, out_shape=[pltpu.VMEM((WX, 2, ROWS, LANES),...  3.11 us
    pallas_call x1, Pallas kernels, body(): pl.pallas_call(update_kernel, out_shape=[jax.ShapeDtypeStruct(square, F32...  1.53 us

profile of v3, /device:TPU:1, one launch (start us, length us, event | category | flops | bytes accessed | tf_op | source)
XLA Modules:
  0.0 48.0 jit_solution(11834295918316236425)
XLA Ops:
  0.6 3.1 %spread.1 = (f32[35,2,80,128]{3,2,1,0:T(8,128)S(1)}, f32[128,128]{1,0:T(8,128)S(1)}, f32[128,128]{1,0:T(8,128)S(1)}, f32[128,128]{1,0:T(8,128)S(1)}) custom-call(s32[128]{0:T(128)} %count_hbm.1, s32[3,128]{1,0:T(4,128)} %base_hbm.3, f32[3]{0:T(128)} %reach_hbm.3, f32[12,16384]{1,0:T(8,128)} %w_hbm.3, f32[128,128]{1,0:T(8,128)} %bitcast.9, f32[128,128]{1,0:T(8,128)} %bitcast.10), custom_call_target="tpu_custom_call" | custom-call | tf_op jit(solution)/shard_map/spread/pallas_call | solution.py:754
  3.7 42.7 %solve.1 = (f32[128,128]{1,0:T(8,128)S(1)}, f32[8,128]{1,0:T(8,128)S(1)}) custom-call(s32[3,128]{1,0:T(4,128)} %base_hbm.3, f32[3]{0:T(128)} %reach_hbm.3, f32[128,128]{1,0:T(8,128)} %bitcast.7, f32[12,16384]{1,0:T(8,128)} %w_hbm.3, f32[35,2,80,128]{3,2,1,0:T(8,128)S(1)} %get-tuple-element.12.grid, f32[128,128]{1,0:T(8,128)S(1)} %get-tuple-element.13.live_dir, ...), custom_call_target="tpu_custom_call" | custom-call | tf_op jit(solution)/shard_map/solve/pallas_call | solution.py:780
  46.5 1.5 %update.1 = (f32[128,128]{1,0:T(8,128)}, f32[128,128]{1,0:T(8,128)}, f32[128,128]{1,0:T(8,128)}) custom-call(f32[128,128]{1,0:T(8,128)} %bitcast.8, f32[8,128]{1,0:T(8,128)S(1)} %get-tuple-element.16.sums, f32[128,128]{1,0:T(8,128)S(1)} %get-tuple-element.15.live, f32[128,128]{1,0:T(8,128)S(1)} %get-tuple-element.13.live_dir, ...), custom_call_target="tpu_custom_call" | custom-call | tf_op jit(solution)/shard_map/update/pallas_call | solution.py:849

commit v4 on v3

--- a/solution.py
+++ b/solution.py
@@ -99,6 +99,7 @@
     live_dir,
     live_res,
     live,
+    lengths,
     table,
     count,
     base,
@@ -136,6 +137,8 @@
     )
     source = iota((136, LANES), 0) - 1
     lane = iota((136, LANES), 1)
+    for i, size in enumerate((NX, NY, NZ)):
+        lengths[i : i + 1, :] = full(reach[i] * float(size))
     table[0] = decay(jnp.abs(lane - 1 - source), length) * scale
     own = (lane >= OWN) & (lane < SPARE)
     second = jnp.where(own, decay(jnp.abs(lane - OWN + NZ - 1 - source), length), 0.0)
@@ -183,17 +186,19 @@
 def solve_kernel(
     sizes,
     base_hbm,
-    reach_hbm,
+    iterate_hbm,
     noise_hbm,
     w_hbm,
+    lengths,
     grid,
     live_dir,
     live_res,
     live,
     image,
     sums,
+    iterate,
     base,
-    reach,
+    spot,
     noise,
     w,
     smooth,
@@ -260,9 +265,8 @@
         pl.semaphore_signal(barrier, inc=1, device_id=at_x(k), device_id_type=MESH)
     for k in range(1, n_yz):
         pl.semaphore_signal(barrier, inc=1, device_id=around_yz(k), device_id_type=MESH)
-    copies_in = fetch(((reach_hbm, reach), (base_hbm, base), (noise_hbm, noise), (w_hbm, w)), in_sem)
-    copies_in[0].wait()
-    length_x, length_y, length_z = reach[0] * float(NX), reach[1] * float(NY), reach[2] * float(NZ)
+    copies_in = fetch(((base_hbm, base), (noise_hbm, noise), (w_hbm, w), (iterate_hbm, iterate)), in_sem)
+    length_x, length_y, length_z = (lengths[i : i + 1, 0:1] for i in range(3))
     sent = []
 
     def chunk(c):
@@ -330,7 +334,7 @@
                     state = step_x * (state + grid[x, half, rows, :])
         return carry
 
-    lax.fori_loop(0, YT, scan, 0)
+    lax.fori_loop(0, YT, scan, 0, unroll=3)
     for x in range(WX):
         for half in range(2):
             smooth[x, half, LIVE:ROWS, :] = jnp.zeros((ROWS - LIVE, LANES), F32)
@@ -397,32 +401,25 @@
 
     lax.fori_loop(2, WX - 3, contract_step, 0, unroll=5)
 
-    def received(dst, sems, slot):
-        pltpu.make_async_remote_copy(
-            src_ref=dst,
-            dst_ref=dst,
-            send_sem=sems.at[0, slot],
-            recv_sem=sems.at[1, slot],
-            device_id={"gx": slot},
-            device_id_type=MESH,
-        ).wait_recv()
-
-    ratio = jnp.exp(full(-float(NX)) / length_x)
-
-    @pl.when(px < OWNERS)
-    def _():
-        x_in[px] = x_out[0:2, chunk(px), :]
-        for p in range(n_gx):
-            pl.when(px != p)(lambda: received(x_in.at[p], x_sem, p))
-        for side, order in enumerate((range(n_gx), reversed(range(n_gx)))):
-            total = jnp.zeros((8, LANES), F32)
-            for q in order:
-                x_prefix[q, side] = total
-                total = total * ratio + x_in[q, side]
-        x_far[:, chunk(px), :] = x_prefix[px]
-        for q in range(n_gx):
-            pl.when(px != q)(back(q).start)
-
+    contract_own(WX - 3)
+    stacks = [jnp.zeros((8, LANES), F32) for _ in range(STACKS)]
+
+    def stacked_planes(planes):
+        for x in planes:
+            for yt in range(YT):
+                stack, copy = divmod(x * YT + yt, COPIES)
+                stacks[stack] = jnp.where(copy_of == copy, smooth[x, 1, 8 * yt : 8 * yt + 8, :], stacks[stack])
+
+    stacked_planes(range(2, WX - 2))
+    copies_in[0].wait()
+
+    def locate(t, carry):
+        spot[0, t] = jnp.clip(base[0, t] - px * NX + 1, 0, NX - 1)
+        spot[1, t] = jnp.clip(base[1, t] - py * NY + 1, 0, NY - 1) + TOP
+        spot[2, t] = jnp.clip(base[2, t] - pz * NZ + 1, 0, NZ - 1)
+        return carry
+
+    lax.fori_loop(0, TILES, locate, 0, unroll=8)
     if n_gx > 1:
         pl.when(px > 0)(x_right.wait_recv)
         pl.when(px + 1 < n_gx)(x_left.wait_recv)
@@ -432,14 +429,10 @@
             packed = jnp.where(valid, x_fix_in[side, kind, LIVE:ROWS, :], 0.0)
             for yt in range(YT):
                 smooth[x, 1, 8 * yt : 8 * yt + 8, :] += unpack(packed, yt)
-    for x in (0, 1, WX - 3, WX - 2, WX - 1):
+    for x in (0, 1, WX - 2, WX - 1):
         contract_own(x)
 
-    stacks = [jnp.zeros((8, LANES), F32) for _ in range(STACKS)]
-    for j in range(WX * YT):
-        x, yt = divmod(j, YT)
-        stack, copy = divmod(j, COPIES)
-        stacks[stack] = jnp.where(copy_of == copy, smooth[x, 1, 8 * yt : 8 * yt + 8, :], stacks[stack])
+    stacked_planes((0, 1, WX - 2, WX - 1))
     for pair in range(PAIRS):
         one, two = stacks[2 * pair], stacks[2 * pair + 1]
         z_out[0, pair] = jnp.where(first_kinds, one, pltpu.roll(two, 3, 1))
@@ -474,6 +467,32 @@
             d_copies[ky, kz] = send(
                 diagonal.at[way(py, ky, n_gy)], diagonal_in.at[index], d_sem, index, at_yz(ky, kz)
             )
+
+    def received(dst, sems, slot):
+        pltpu.make_async_remote_copy(
+            src_ref=dst,
+            dst_ref=dst,
+            send_sem=sems.at[0, slot],
+            recv_sem=sems.at[1, slot],
+            device_id={"gx": slot},
+            device_id_type=MESH,
+        ).wait_recv()
+
+    ratio = jnp.exp(full(-float(NX)) / length_x)
+
+    @pl.when(px < OWNERS)
+    def _():
+        x_in[px] = x_out[0:2, chunk(px), :]
+        for p in range(n_gx):
+            pl.when(px != p)(lambda: received(x_in.at[p], x_sem, p))
+        for side, order in enumerate((range(n_gx), reversed(range(n_gx)))):
+            total = jnp.zeros((8, LANES), F32)
+            for q in order:
+                x_prefix[q, side] = total
+                total = total * ratio + x_in[q, side]
+        x_far[:, chunk(px), :] = x_prefix[px]
+        for q in range(n_gx):
+            pl.when(px != q)(back(q).start)
 
     cell = iota((136, LANES), 0) - 1
     wide = iota((136, LANES), 1)
@@ -595,16 +614,13 @@
                 smooth[x, half, rows, :] = value
         return carry
 
-    lax.fori_loop(0, WX, expand, 0)
+    lax.fori_loop(0, WX, expand, 0, unroll=5)
     for copy in copies_in[1:]:
         copy.wait()
 
     def tile_spot(t):
         at = pl.ds(pl.multiple_of(t * LANES, LANES), LANES)
-        x0 = jnp.clip(base[0, t] - px * NX + 1, 0, NX - 1)
-        y0 = jnp.clip(base[1, t] - py * NY + 1, 0, NY - 1) + TOP
-        z0 = jnp.clip(base[2, t] - pz * NZ + 1, 0, NZ - 1)
-        return at, x0, y0, z0
+        return at, spot[0, t], spot[1, t], spot[2, t]
 
     def gather(rows, weights, at, z0):
         total = None
@@ -697,11 +713,13 @@
         (live_res[...], value),
         (value, value),
     )
-    sum_out[...] = jnp.concatenate(
-        [jnp.sum(a * b, axis=0, keepdims=True) for a, b in pairs] + [jnp.zeros((4, LANES), F32)], axis=0
-    )
+    place = iota((1, LANES), 1)
+    total = jnp.zeros((1, LANES), F32)
+    for i, (a, b) in enumerate(pairs):
+        part = jnp.sum(jnp.sum(a * b, axis=0, keepdims=True), axis=1, keepdims=True)
+        total = jnp.where(place == i, part, total)
+    sum_out[...] = total
     copies = [send(sum_out, sum_in_x.at[k - 1], sx_sem, k - 1, at_x(k)) for k in range(1, n_gx)]
-    total = sum_out[...]
     for k in range(1, n_gx):
         copies[k - 1].wait_recv()
         total = total + sum_in_x[k - 1]
@@ -720,18 +738,16 @@
             pl.when(px != q)(back(q).wait_send)
 
 
-def update_kernel(
-    iterate_hbm, sums, live, live_dir, live_res, image, new_iterate, new_residual, new_direction, iterate, sem
-):
-    copies = fetch(((iterate_hbm, iterate),), sem)
-    def total(row):
-        return jnp.sum(sums[row : row + 1, :], axis=1, keepdims=True)
+def update_kernel(sums, iterate, live, live_dir, live_res, image, new_iterate, new_residual, new_direction):
+    place = iota((1, LANES), 1)
+
+    def total(which):
+        return jnp.sum(jnp.where(place == which, sums[...], 0.0), axis=1, keepdims=True)
 
     norm_old, curvature, cross, square = total(0), total(1), total(2), total(3)
     step = norm_old / curvature
     norm_new = norm_old + step * (step * square - 2.0 * cross)
     held = live_res[...] - step * image[...]
-    copies[0].wait()
     new_iterate[...] = live[...] * iterate[...] + step * live_dir[...]
     new_residual[...] = held
     new_direction[...] = held + norm_new / norm_old * live_dir[...]
@@ -751,11 +767,11 @@
     def keep(x):
         return pltpu.with_memory_space_constraint(x, pltpu.VMEM)
 
-    grid, live_dir, live_res, live = pl.pallas_call(
+    grid, live_dir, live_res, live, lengths = pl.pallas_call(
         spread_kernel,
-        out_shape=[pltpu.VMEM((WX, 2, ROWS, LANES), F32)] + [pltpu.VMEM(square, F32)] * 3,
+        out_shape=[pltpu.VMEM((WX, 2, ROWS, LANES), F32)] + [pltpu.VMEM(square, F32)] * 3 + [pltpu.VMEM((8, LANES), F32)],
         in_specs=[in_hbm] * 6,
-        out_specs=[in_vmem] * 4,
+        out_specs=[in_vmem] * 5,
         scratch_shapes=[
             pltpu.VMEM((2, 136, LANES), F32),
             pltpu.SMEM((TILES,), jnp.int32),
@@ -777,14 +793,14 @@
         away(residual.reshape(square)),
     )
 
-    image, sums = pl.pallas_call(
+    image, sums, kept = pl.pallas_call(
         functools.partial(solve_kernel, sizes),
-        out_shape=[pltpu.VMEM(square, F32), pltpu.VMEM((8, LANES), F32)],
-        in_specs=[in_hbm] * 4 + [in_vmem] * 4,
-        out_specs=[in_vmem] * 2,
+        out_shape=[pltpu.VMEM(square, F32), pltpu.VMEM((1, LANES), F32), pltpu.VMEM(square, F32)],
+        in_specs=[in_hbm] * 4 + [in_vmem] * 5,
+        out_specs=[in_vmem] * 3,
         scratch_shapes=[
             pltpu.SMEM((3, TILES), jnp.int32),
-            pltpu.SMEM((3,), F32),
+            pltpu.SMEM((3, TILES), jnp.int32),
             pltpu.VMEM(square, F32),
             pltpu.VMEM((12, TILES * LANES), F32),
             pltpu.VMEM((WX, 2, ROWS, LANES), F32),
@@ -814,10 +830,10 @@
             pltpu.VMEM((3, 8, LANES), F32),
             pltpu.VMEM((12, 2, 8, LANES), F32),
             pltpu.VMEM(square, F32),
-            pltpu.VMEM((8, LANES), F32),
-            pltpu.VMEM((15, 8, LANES), F32),
-            pltpu.VMEM((8, LANES), F32),
-            pltpu.VMEM((15, 8, LANES), F32),
+            pltpu.VMEM((1, LANES), F32),
+            pltpu.VMEM((15, 1, LANES), F32),
+            pltpu.VMEM((1, LANES), F32),
+            pltpu.VMEM((15, 1, LANES), F32),
             dma((4,)),
             dma((2, n_gx)),
             dma((2, n_gx)),
@@ -837,9 +853,10 @@
         name="solve",
     )(
         away(stencil_base),
-        away(reach),
+        away(iterate.reshape(square)),
         away(noise.reshape(square)),
         away(interp_weights),
+        keep(lengths),
         keep(grid),
         keep(live_dir),
         keep(live_res),
@@ -849,11 +866,10 @@
     outs = pl.pallas_call(
         update_kernel,
         out_shape=[jax.ShapeDtypeStruct(square, F32)] * 3,
-        in_specs=[in_hbm] + [in_vmem] * 5,
+        in_specs=[in_vmem] * 6,
         out_specs=[in_vmem] * 3,
-        scratch_shapes=[pltpu.VMEM(square, F32), dma((1,))],
         name="update",
-    )(away(iterate.reshape(square)), keep(sums), keep(live), keep(live_dir), keep(live_res), keep(image))
+    )(keep(sums), keep(kept), keep(live), keep(live_dir), keep(live_res), keep(image))
     return tuple(out.reshape(-1) for out in outs)
 
 

time: 48.2 us -> 44.8 us (0.929)
  Pallas kernels: 47.4 us -> 44 us
    pallas_call x1, Pallas kernels: 42.7 us -> 40.1 us  [body(): pl.pallas_call(functools.partial(solve_kernel, sizes), out_shape=[pltpu.V...]
    pallas_call x1, Pallas kernels: 1.53 us -> 0.77 us  [body(): pl.pallas_call(update_kernel, out_shape=[jax.ShapeDtypeStruct(square, F32...]
where the time goes in v4:
time: 44.8 us; the launch traced here: 44.7 us
  Pallas kernels  44 us (98%)
  between operations  0.65 us (1%)
    pallas_call x1, Pallas kernels, body(): pl.pallas_call(functools.partial(solve_kernel, sizes), out_shape=[pltpu.V...  40.1 us
    pallas_call x1, Pallas kernels, body(): pl.pallas_call(spread_kernel, out_shape=[pltpu.VMEM((WX, 2, ROWS, LANES),...  3.12 us

profile of v4, /device:TPU:1, one launch (start us, length us, event | category | flops | bytes accessed | tf_op | source)
XLA Modules:
  0.0 44.7 jit_solution(6761975323006948965)
XLA Ops:
  0.6 3.1 %spread.1 = (f32[35,2,80,128]{3,2,1,0:T(8,128)S(1)}, f32[128,128]{1,0:T(8,128)S(1)}, f32[128,128]{1,0:T(8,128)S(1)}, f32[128,128]{1,0:T(8,128)S(1)}, f32[8,128]{1,0:T(8,128)S(1)}) custom-call(s32[128]{0:T(128)} %count_hbm.1, s32[3,128]{1,0:T(4,128)} %base_hbm.3, f32[3]{0:T(128)} %reach_hbm.1, f32[12,16384]{1,0:T(8,128)} %w_hbm.3, f32[128,128]{1,0:T(8,128)} %bitcast.9, ...), custom_call_target="tpu_custom_call" | custom-call | tf_op jit(solution)/shard_map/spread/pallas_call | solution.py:770
  3.8 40.1 %solve.1 = (f32[128,128]{1,0:T(8,128)S(1)}, f32[1,128]{1,0:T(1,128)S(1)}, f32[128,128]{1,0:T(8,128)S(1)}) custom-call(s32[3,128]{1,0:T(4,128)} %base_hbm.3, f32[128,128]{1,0:T(8,128)} %bitcast.7, f32[128,128]{1,0:T(8,128)} %bitcast.8, f32[12,16384]{1,0:T(8,128)} %w_hbm.3, f32[8,128]{1,0:T(8,128)S(1)} %get-tuple-element.14.lengths, ...), custom_call_target="tpu_custom_call" | custom-call | tf_op jit(solution)/shard_map/solve/pallas_call | solution.py:796
  43.9 0.8 %update.1 = (f32[128,128]{1,0:T(8,128)}, f32[128,128]{1,0:T(8,128)}, f32[128,128]{1,0:T(8,128)}) custom-call(f32[1,128]{1,0:T(1,128)S(1)} %get-tuple-element.19.sums, f32[128,128]{1,0:T(8,128)S(1)} %get-tuple-element.20.iterate, f32[128,128]{1,0:T(8,128)S(1)} %get-tuple-element.18.live, f32[128,128]{1,0:T(8,128)S(1)} %get-tuple-element.16.live_dir, ...), custom_call_target="tpu_custom_call" | custom-call | tf_op jit(solution)/shard_map/update/pallas_call | solution.py:866

commit v5 on v4

--- a/solution.py
+++ b/solution.py
@@ -22,7 +22,7 @@
 PAIRS = STACKS // 2
 XROWS = 40
 SIDE, FIX = XROWS, XROWS + 8
-YMSG = FIX + 2 * XROWS
+SPLIT = 24
 PACK = SPARE + CHANNELS - OWN
 OWNERS = ROWS // 8
 MESH = pl.DeviceIdType.MESH
@@ -72,6 +72,14 @@
     place = jnp.maximum(lane - SPARE, 0)
     copy = place // CHANNELS
     return jnp.where(spare, place - copy * CHANNELS, -1), jnp.where(spare, copy, -1)
+
+
+def line_row(x):
+    return (x + XROWS - 8) % XROWS
+
+
+def pair_place(pair):
+    return {0: PAIRS - 2, PAIRS - 1: PAIRS - 1}.get(pair, pair - 1)
 
 
 def tile_weights(w8, low):
@@ -180,7 +188,7 @@
                 grid[spot] = grid[spot] + jnp.where(keep, parts[a // 2][half], 0.0)
         return carry
 
-    lax.fori_loop(0, TILES, tile, 0, unroll=16)
+    lax.fori_loop(0, TILES, tile, 0, unroll=32)
 
 
 def solve_kernel(
@@ -213,6 +221,7 @@
     x_far,
     x_fix_in,
     y_msg,
+    y_fix,
     y_side,
     diagonal,
     z_out,
@@ -227,6 +236,8 @@
     far_y,
     far_z_in,
     far_y_in,
+    near_weight,
+    far_weight,
     sampled,
     sum_out,
     sum_in_x,
@@ -311,33 +322,23 @@
     fix_one = step_x - jnp.exp(full(1.0) / length_x)
     fix_two = jnp.exp(full(-2.0) / length_x) - jnp.exp(full(2.0) / length_x)
 
-    def scan(yt, carry):
+    def moments(yt, carry):
         rows = pl.ds(pl.multiple_of(yt * 8, 8), 8)
         for half, out in enumerate((x_out, x_side)):
-            state = grid[0, half, rows, :]
-            smooth[0, half, rows, :] = state
+            edge = [grid[x, half, rows, :] for x in (0, 1, WX - 2, WX - 1)]
+            up, down = edge[0], edge[3]
             for x in range(1, WX):
-                state = grid[x, half, rows, :] + step_x * state
-                smooth[x, half, rows, :] = state
-            out[0, rows, :] = state
-            edge = [grid[x, half, rows, :] for x in (0, 1, WX - 2, WX - 1)]
+                up = grid[x, half, rows, :] + step_x * up
+                down = grid[WX - 1 - x, half, rows, :] + step_x * down
+            out[0, rows, :] = up
+            out[1, rows, :] = down
             out[2, rows, :] = edge[2] * fix_one + edge[3] * fix_two
             out[3, rows, :] = edge[3] * fix_one
             out[4, rows, :] = edge[0] * fix_two + edge[1] * fix_one
             out[5, rows, :] = edge[0] * fix_one
-            state = step_x * edge[3]
-            for x in reversed(range(WX - 1)):
-                smooth[x, half, rows, :] = smooth[x, half, rows, :] + state
-                if x == 0:
-                    out[1, rows, :] = state + edge[0]
-                else:
-                    state = step_x * (state + grid[x, half, rows, :])
         return carry
 
-    lax.fori_loop(0, YT, scan, 0, unroll=3)
-    for x in range(WX):
-        for half in range(2):
-            smooth[x, half, LIVE:ROWS, :] = jnp.zeros((ROWS - LIVE, LANES), F32)
+    lax.fori_loop(0, YT, moments, 0, unroll=3)
     for plane in range(6):
         total = jnp.zeros((8, LANES), F32)
         for yt in range(YT):
@@ -354,6 +355,26 @@
     x_left = send(x_out.at[pl.ds(4, 2)], x_fix_in.at[1], x_fix_sem, 1, at_x(n_gx - 1), px > 0)
     for c in range(OWNERS):
         send(x_out.at[pl.ds(0, 2), chunk(c), :], x_in.at[px], x_sem, c, {"gx": c}, px != c, px)
+
+    def scan(yt, carry):
+        rows = pl.ds(pl.multiple_of(yt * 8, 8), 8)
+        for half in range(2):
+            state = grid[0, half, rows, :]
+            smooth[0, half, rows, :] = state
+            for x in range(1, WX):
+                state = grid[x, half, rows, :] + step_x * state
+                smooth[x, half, rows, :] = state
+            state = step_x * grid[WX - 1, half, rows, :]
+            for x in reversed(range(WX - 1)):
+                smooth[x, half, rows, :] = smooth[x, half, rows, :] + state
+                if x > 0:
+                    state = step_x * (state + grid[x, half, rows, :])
+        return carry
+
+    lax.fori_loop(0, YT, scan, 0, unroll=3)
+    for x in range(WX):
+        for half in range(2):
+            smooth[x, half, LIVE:ROWS, :] = jnp.zeros((ROWS - LIVE, LANES), F32)
 
     row = iota((96, 3 * ROWS), 0)
     col = iota((96, 3 * ROWS), 1)
@@ -391,9 +412,12 @@
         for side in range(2):
             for kind in range(3):
                 line = result[ROWS + 4 * side + kind : ROWS + 4 * side + kind + 1]
-                start = 0 if kind == 0 else FIX + XROWS * (kind - 1)
-                y_msg[side, pl.ds(start + x, 1), :] = line[:, :LANES]
-                y_side[side, kind, pl.ds(x, 1), :] = line[:, LANES:]
+                at = pl.ds(line_row(x), 1)
+                if kind == 0:
+                    y_msg[side, at, :] = line[:, :LANES]
+                else:
+                    y_fix[side, kind - 1, at, :] = line[:, :LANES]
+                y_side[side, kind, at, :] = line[:, LANES:]
 
     def contract_step(x, carry):
         contract_own(x)
@@ -410,63 +434,38 @@
                 stack, copy = divmod(x * YT + yt, COPIES)
                 stacks[stack] = jnp.where(copy_of == copy, smooth[x, 1, 8 * yt : 8 * yt + 8, :], stacks[stack])
 
+    def pair_up(pair):
+        one, two = stacks[2 * pair], stacks[2 * pair + 1]
+        z_out[0, pair_place(pair)] = jnp.where(first_kinds, one, pltpu.roll(two, 3, 1))
+        z_out[1, pair_place(pair)] = jnp.where(first_kinds, pltpu.roll(one, LANES - 3, 1), two)
+
+    early, late = pl.ds(0, PAIRS - 2), pl.ds(PAIRS - 2, 2)
+    full_rows, rest_rows, rest_fix = pl.ds(0, SPLIT), pl.ds(SPLIT, FIX - SPLIT), pl.ds(SPLIT, XROWS - SPLIT)
     stacked_planes(range(2, WX - 2))
-    copies_in[0].wait()
-
-    def locate(t, carry):
-        spot[0, t] = jnp.clip(base[0, t] - px * NX + 1, 0, NX - 1)
-        spot[1, t] = jnp.clip(base[1, t] - py * NY + 1, 0, NY - 1) + TOP
-        spot[2, t] = jnp.clip(base[2, t] - pz * NZ + 1, 0, NZ - 1)
-        return carry
-
-    lax.fori_loop(0, TILES, locate, 0, unroll=8)
-    if n_gx > 1:
-        pl.when(px > 0)(x_right.wait_recv)
-        pl.when(px + 1 < n_gx)(x_left.wait_recv)
-    for side, valid, places in ((0, px > 0, (0, 1)), (1, px + 1 < n_gx, (WX - 1, WX - 2))):
-        for kind, x in enumerate(places):
-            smooth[x, 0, 0:LIVE, :] += jnp.where(valid, x_fix_in[side, kind, 0:LIVE, :], 0.0)
-            packed = jnp.where(valid, x_fix_in[side, kind, LIVE:ROWS, :], 0.0)
-            for yt in range(YT):
-                smooth[x, 1, 8 * yt : 8 * yt + 8, :] += unpack(packed, yt)
-    for x in (0, 1, WX - 2, WX - 1):
-        contract_own(x)
-
-    stacked_planes((0, 1, WX - 2, WX - 1))
-    for pair in range(PAIRS):
-        one, two = stacks[2 * pair], stacks[2 * pair + 1]
-        z_out[0, pair] = jnp.where(first_kinds, one, pltpu.roll(two, 3, 1))
-        z_out[1, pair] = jnp.where(first_kinds, pltpu.roll(one, LANES - 3, 1), two)
-    for side in range(2):
-        beside = jnp.zeros((8, LANES), F32)
-        both = jnp.zeros((8, LANES), F32)
-        for j in range(15):
-            kind, xt = divmod(j, 5)
-            value = y_side[side, kind, 8 * xt : 8 * xt + 8, :]
-            moved = pltpu.roll(value, 8 * j, 1) if j else value
-            beside = jnp.where((lane >= 8 * j) & (lane < 8 * j + 8), moved, beside)
-            both = jnp.where(copy_of == j, value, both)
-        y_msg[side, SIDE : SIDE + 8, :] = beside
-        diagonal[side] = both
+    for pair in range(1, PAIRS - 1):
+        pair_up(pair)
     z_copies = [
-        send(z_out.at[way(pz, k, n_gz)], z_in.at[k - 1], z_sem, k - 1, at_yz(0, k)) for k in range(1, n_gz)
+        send(z_out.at[way(pz, k, n_gz), early], z_in.at[k - 1, early], z_sem, k - 1, at_yz(0, k))
+        for k in range(1, n_gz)
     ]
+
     y_copies = [
-        send(y_msg.at[way(py, k, n_gy), pl.ds(0, FIX), :], y_in.at[k - 1], y_sem, k - 1, at_yz(k, 0))
+        send(y_msg.at[way(py, k, n_gy), full_rows], y_in.at[k - 1, full_rows], y_sem, k - 1, at_yz(k, 0))
         for k in range(1, n_gy)
     ]
-    y_right = y_left = None
-    if n_gy > 1:
-        fixes = pl.ds(FIX, 2 * XROWS)
-        y_right = send(y_msg.at[0, fixes, :], y_fix_in.at[0], y_fix_sem, 0, at_yz(1, 0), py + 1 < n_gy)
-        y_left = send(y_msg.at[1, fixes, :], y_fix_in.at[1], y_fix_sem, 1, at_yz(n_gy - 1, 0), py > 0)
-    d_copies = {}
-    for ky in range(1, n_gy):
-        for kz in range(1, n_gz):
-            index = (ky - 1) * (n_gz - 1) + kz - 1
-            d_copies[ky, kz] = send(
-                diagonal.at[way(py, ky, n_gy)], diagonal_in.at[index], d_sem, index, at_yz(ky, kz)
+    y_fixes = []
+
+    def send_fixes(rows, index):
+        if n_gy > 1:
+            right = send(
+                y_fix.at[0, :, rows], y_fix_in.at[0, :, rows], y_fix_sem, index, at_yz(1, 0), py + 1 < n_gy
             )
+            left = send(
+                y_fix.at[1, :, rows], y_fix_in.at[1, :, rows], y_fix_sem, index + 1, at_yz(n_gy - 1, 0), py > 0
+            )
+            y_fixes.append((right, left))
+
+    send_fixes(full_rows, 0)
 
     def received(dst, sems, slot):
         pltpu.make_async_remote_copy(
@@ -493,6 +492,59 @@
         x_far[:, chunk(px), :] = x_prefix[px]
         for q in range(n_gx):
             pl.when(px != q)(back(q).start)
+
+    if n_gx > 1:
+        pl.when(px > 0)(x_right.wait_recv)
+        pl.when(px + 1 < n_gx)(x_left.wait_recv)
+    for side, valid, places in ((0, px > 0, (0, 1)), (1, px + 1 < n_gx, (WX - 1, WX - 2))):
+        for kind, x in enumerate(places):
+            smooth[x, 0, 0:LIVE, :] += jnp.where(valid, x_fix_in[side, kind, 0:LIVE, :], 0.0)
+            packed = jnp.where(valid, x_fix_in[side, kind, LIVE:ROWS, :], 0.0)
+            for yt in range(YT):
+                smooth[x, 1, 8 * yt : 8 * yt + 8, :] += unpack(packed, yt)
+    for x in (0, 1, WX - 2, WX - 1):
+        contract_own(x)
+
+    stacked_planes((0, 1, WX - 2, WX - 1))
+    pair_up(0)
+    pair_up(PAIRS - 1)
+    for side in range(2):
+        beside = jnp.zeros((8, LANES), F32)
+        both = jnp.zeros((8, LANES), F32)
+        for j in range(15):
+            kind, xt = divmod(j, 5)
+            value = y_side[side, kind, 8 * xt : 8 * xt + 8, :]
+            moved = pltpu.roll(value, 8 * j, 1) if j else value
+            beside = jnp.where((lane >= 8 * j) & (lane < 8 * j + 8), moved, beside)
+            both = jnp.where(copy_of == j, value, both)
+        y_msg[side, SIDE : SIDE + 8, :] = beside
+        diagonal[side] = both
+    z_copies += [
+        send(z_out.at[way(pz, k, n_gz), late], z_in.at[k - 1, late], z_sem, k + 2, at_yz(0, k))
+        for k in range(1, n_gz)
+    ]
+    y_copies += [
+        send(y_msg.at[way(py, k, n_gy), rest_rows], y_in.at[k - 1, rest_rows], y_sem, k + 2, at_yz(k, 0))
+        for k in range(1, n_gy)
+    ]
+    send_fixes(rest_fix, 2)
+    d_copies = {}
+    for ky in range(1, n_gy):
+        for kz in range(1, n_gz):
+            index = (ky - 1) * (n_gz - 1) + kz - 1
+            d_copies[ky, kz] = send(
+                diagonal.at[way(py, ky, n_gy)], diagonal_in.at[index], d_sem, index, at_yz(ky, kz)
+            )
+
+    copies_in[0].wait()
+
+    def locate(t, carry):
+        spot[0, t] = jnp.clip(base[0, t] - px * NX + 1, 0, NX - 1)
+        spot[1, t] = jnp.clip(base[1, t] - py * NY + 1, 0, NY - 1) + TOP
+        spot[2, t] = jnp.clip(base[2, t] - pz * NZ + 1, 0, NZ - 1)
+        return carry
+
+    lax.fori_loop(0, TILES, locate, 0, unroll=8)
 
     cell = iota((136, LANES), 0) - 1
     wide = iota((136, LANES), 1)
@@ -508,6 +560,26 @@
     cell = iota((ROWS, LANES), 0) - TOP - 1
     for side in range(2):
         pick_y[side] = incoming(3 * side, cell, NY, length_y)
+
+    for copy in copies_in[1:]:
+        copy.wait()
+
+    def weigh(t, carry):
+        w8 = w[0:8, pl.ds(pl.multiple_of(t * LANES, LANES), LANES)]
+        first, second, along_y = tile_weights(w8, low)
+        along_x = []
+        for side in range(2):
+            total = None
+            for a in range(4):
+                term = w8[a : a + 1] * pick_x[side, pl.ds(spot[0, t] + a, 1), :]
+                total = term if a == 0 else total + term
+            along_x.append(total)
+        near_weight[t, 0:8, :] = first
+        near_weight[t, 8:16, :] = second
+        far_weight[t] = jnp.where(low, along_x[0], along_x[1]) * along_y
+        return carry
+
+    lax.fori_loop(0, TILES, weigh, 0, unroll=8)
 
     for c in range(OWNERS):
         pl.when(px != c)(lambda: received(x_far.at[:, chunk(c), :], x_back_sem, c))
@@ -549,9 +621,10 @@
     from_z = [[jnp.zeros((8, LANES), F32) for _ in range(PAIRS)] for _ in range(2)]
     for k in range(1, n_gz):
         z_copies[k - 1].wait_recv()
+        z_copies[k + n_gz - 2].wait_recv()
         weights = [jnp.where(is_moment, moment, fix) for moment, fix in mix(pz, n_gz, NZ, length_z, k)]
         for pair in range(PAIRS):
-            got = z_in[k - 1, pair]
+            got = z_in[k - 1, pair_place(pair)]
             for side in range(2):
                 from_z[side][pair] = from_z[side][pair] + weights[side] * got
     for pair in range(PAIRS):
@@ -563,6 +636,7 @@
     lines = [[jnp.zeros((8, LANES), F32) for _ in range(XROWS // 8)] for _ in range(2)]
     for ky in range(1, n_gy):
         y_copies[ky - 1].wait_recv()
+        y_copies[ky + n_gy - 2].wait_recv()
         weights = mix(py, n_gy, NY, length_y, ky)
         for side in range(2):
             moment, fix = weights[side]
@@ -575,15 +649,14 @@
             for side in range(2):
                 moment, fix = weights[side]
                 both[side] = both[side] + jnp.where(copy_of < 5, moment, fix) * got
-    if n_gy > 1:
-        pl.when(py > 0)(y_right.wait_recv)
-        pl.when(py + 1 < n_gy)(y_left.wait_recv)
+    for right, left in y_fixes:
+        pl.when(py > 0)(right.wait_recv)
+        pl.when(py + 1 < n_gy)(left.wait_recv)
     for side, valid in enumerate((py > 0, py + 1 < n_gy)):
         for tile in range(XROWS // 8):
             y_mixed[side, 0, 0, 8 * tile : 8 * tile + 8, :] = lines[side][tile]
         for kind in range(1, 3):
-            start = XROWS * (kind - 1)
-            y_mixed[side, kind, 0] = jnp.where(valid, y_fix_in[side, start : start + XROWS, :], 0.0)
+            y_mixed[side, kind, 0] = jnp.where(valid, y_fix_in[side, kind - 1], 0.0)
         for j in range(15):
             kind, xt = divmod(j, 5)
             moved = pltpu.roll(beside[side], LANES - 8 * j, 1) if j else beside[side]
@@ -594,7 +667,7 @@
     def expand(x, carry):
         for half in range(2):
             line = [
-                [y_mixed[side, kind, half, pl.ds(x, 1), :] for kind in range(3)] for side in range(2)
+                [y_mixed[side, kind, half, pl.ds(line_row(x), 1), :] for kind in range(3)] for side in range(2)
             ]
             for yt in range(YT):
                 rows = slice(8 * yt, 8 * yt + 8)
@@ -615,8 +688,6 @@
         return carry
 
     lax.fori_loop(0, WX, expand, 0, unroll=5)
-    for copy in copies_in[1:]:
-        copy.wait()
 
     def tile_spot(t):
         at = pl.ds(pl.multiple_of(t * LANES, LANES), LANES)
@@ -636,7 +707,6 @@
 
     def near(t, carry):
         at, x0, y0, z0 = tile_spot(t)
-        first, second, _ = tile_weights(w[0:8, at], low)
         rows = [
             [
                 jnp.where(
@@ -646,10 +716,10 @@
             ]
             for a in (0, 2)
         ]
-        sampled[pl.ds(t, 1), :] = gather(rows, (first, second), at, z0)
+        sampled[pl.ds(t, 1), :] = gather(rows, (near_weight[t, 0:8, :], near_weight[t, 8:16, :]), at, z0)
         return carry
 
-    lax.fori_loop(0, TILES, near, 0, unroll=16)
+    lax.fori_loop(0, TILES, near, 0, unroll=32)
 
     from_z = jnp.zeros((8, LANES), F32)
     for k in range(1, n_gz):
@@ -689,21 +759,11 @@
 
     def distant(t, carry):
         at, x0, y0, z0 = tile_spot(t)
-        w8 = w[0:8, at]
-        _, _, along_y = tile_weights(w8, low)
-        along_x = []
-        for side in range(2):
-            total = None
-            for a in range(4):
-                term = w8[a : a + 1] * pick_x[side, pl.ds(x0 + a, 1), :]
-                total = term if a == 0 else total + term
-            along_x.append(total)
-        weight = jnp.where(low, along_x[0], along_x[1]) * along_y
         rows = [jnp.where(low, far[0, half, pl.ds(y0, 8), :], far[1, half, pl.ds(y0 - 4, 8), :]) for half in range(2)]
-        sampled[pl.ds(t, 1), :] += gather([rows], [weight], at, z0)
+        sampled[pl.ds(t, 1), :] += gather([rows], [far_weight[t]], at, z0)
         return carry
 
-    lax.fori_loop(0, TILES, distant, 0, unroll=16)
+    lax.fori_loop(0, TILES, distant, 0, unroll=32)
 
     value = live[...] * (sampled[...] + noise[...] * live_dir[...])
     image[...] = value
@@ -814,13 +874,14 @@
             pltpu.VMEM((n_gx, 2, 8, LANES), F32),
             pltpu.VMEM((2, ROWS, LANES), F32),
             pltpu.VMEM((2, 2, ROWS, LANES), F32),
-            pltpu.VMEM((2, YMSG, LANES), F32),
+            pltpu.VMEM((2, FIX, LANES), F32),
+            pltpu.VMEM((2, 2, XROWS, LANES), F32),
             pltpu.VMEM((2, 3, XROWS, LANES), F32),
             pltpu.VMEM((2, 8, LANES), F32),
             pltpu.VMEM((2, PAIRS, 8, LANES), F32),
             pltpu.VMEM((3, PAIRS, 8, LANES), F32),
             pltpu.VMEM((3, FIX, LANES), F32),
-            pltpu.VMEM((2, 2 * XROWS, LANES), F32),
+            pltpu.VMEM((2, 2, XROWS, LANES), F32),
             pltpu.VMEM((9, 8, LANES), F32),
             pltpu.VMEM((STACKS, 8, LANES), F32),
             pltpu.VMEM((2, 3, 2, XROWS, LANES), F32),
@@ -829,6 +890,8 @@
             pltpu.VMEM((2, 2, 8, LANES), F32),
             pltpu.VMEM((3, 8, LANES), F32),
             pltpu.VMEM((12, 2, 8, LANES), F32),
+            pltpu.VMEM((TILES, 16, LANES), F32),
+            pltpu.VMEM((TILES, 8, LANES), F32),
             pltpu.VMEM(square, F32),
             pltpu.VMEM((1, LANES), F32),
             pltpu.VMEM((15, 1, LANES), F32),
@@ -838,9 +901,9 @@
             dma((2, n_gx)),
             dma((2, n_gx)),
             dma((2, 2)),
-            dma((2, 3)),
-            dma((2, 3)),
-            dma((2, 2)),
+            dma((2, 6)),
+            dma((2, 6)),
+            dma((2, 4)),
             dma((2, 9)),
             dma((2, 3)),
             dma((2, 12)),

time: 44.8 us -> 44.1 us (0.984)
  Pallas kernels: 44 us -> 43.4 us
where the time goes in v5:
time: 44.1 us; the launch traced here: 44 us
  Pallas kernels  43.4 us (98%)
  between operations  0.65 us (1%)
    pallas_call x1, Pallas kernels, body(): pl.pallas_call(functools.partial(solve_kernel, sizes), out_shape=[pltpu.V...  39.7 us
    pallas_call x1, Pallas kernels, body(): pl.pallas_call(spread_kernel, out_shape=[pltpu.VMEM((WX, 2, ROWS, LANES),...  2.9 us

profile of v5, /device:TPU:1, one launch (start us, length us, event | category | flops | bytes accessed | tf_op | source)
XLA Modules:
  0.0 44.0 jit_solution(1890613902049249481)
XLA Ops:
  0.6 2.9 %spread.1 = (f32[35,2,80,128]{3,2,1,0:T(8,128)S(1)}, f32[128,128]{1,0:T(8,128)S(1)}, f32[128,128]{1,0:T(8,128)S(1)}, f32[128,128]{1,0:T(8,128)S(1)}, f32[8,128]{1,0:T(8,128)S(1)}) custom-call(s32[128]{0:T(128)} %count_hbm.1, s32[3,128]{1,0:T(4,128)} %base_hbm.3, f32[3]{0:T(128)} %reach_hbm.1, f32[12,16384]{1,0:T(8,128)} %w_hbm.3, f32[128,128]{1,0:T(8,128)} %bitcast.9, ...), custom_call_target="tpu_custom_call" | custom-call | tf_op jit(solution)/shard_map/spread/pallas_call | solution.py:830
  3.5 39.7 %solve.1 = (f32[128,128]{1,0:T(8,128)S(1)}, f32[1,128]{1,0:T(1,128)S(1)}, f32[128,128]{1,0:T(8,128)S(1)}) custom-call(s32[3,128]{1,0:T(4,128)} %base_hbm.3, f32[128,128]{1,0:T(8,128)} %bitcast.7, f32[128,128]{1,0:T(8,128)} %bitcast.8, f32[12,16384]{1,0:T(8,128)} %w_hbm.3, f32[8,128]{1,0:T(8,128)S(1)} %get-tuple-element.14.lengths, ...), custom_call_target="tpu_custom_call" | custom-call | tf_op jit(solution)/shard_map/solve/pallas_call | solution.py:856
  43.2 0.8 %update.1 = (f32[128,128]{1,0:T(8,128)}, f32[128,128]{1,0:T(8,128)}, f32[128,128]{1,0:T(8,128)}) custom-call(f32[1,128]{1,0:T(1,128)S(1)} %get-tuple-element.19.sums, f32[128,128]{1,0:T(8,128)S(1)} %get-tuple-element.20.iterate, f32[128,128]{1,0:T(8,128)S(1)} %get-tuple-element.18.live, f32[128,128]{1,0:T(8,128)S(1)} %get-tuple-element.16.live_dir, ...), custom_call_target="tpu_custom_call" | custom-call | tf_op jit(solution)/shard_map/update/pallas_call | solution.py:929

commit v6 on v5

--- a/solution.py
+++ b/solution.py
@@ -779,15 +779,15 @@
         part = jnp.sum(jnp.sum(a * b, axis=0, keepdims=True), axis=1, keepdims=True)
         total = jnp.where(place == i, part, total)
     sum_out[...] = total
-    copies = [send(sum_out, sum_in_x.at[k - 1], sx_sem, k - 1, at_x(k)) for k in range(1, n_gx)]
+    copies = [send(sum_out, sum_in_yz.at[k - 1], syz_sem, k - 1, around_yz(k)) for k in range(1, n_yz)]
+    for k in range(1, n_yz):
+        copies[k - 1].wait_recv()
+        total = total + sum_in_yz[k - 1]
+    sum_mid[...] = total
+    copies = [send(sum_mid, sum_in_x.at[k - 1], sx_sem, k - 1, at_x(k)) for k in range(1, n_gx)]
     for k in range(1, n_gx):
         copies[k - 1].wait_recv()
         total = total + sum_in_x[k - 1]
-    sum_mid[...] = total
-    copies = [send(sum_mid, sum_in_yz.at[k - 1], syz_sem, k - 1, around_yz(k)) for k in range(1, n_yz)]
-    for k in range(1, n_yz):
-        copies[k - 1].wait_recv()
-        total = total + sum_in_yz[k - 1]
     sums[...] = total
     for wait in sent:
         wait()

time: 44.1 us -> 43.3 us (0.982)
  Pallas kernels: 43.4 us -> 42.5 us
    pallas_call x1, Pallas kernels: 39.7 us -> 38.8 us  [body(): pl.pallas_call(functools.partial(solve_kernel, sizes), out_shape=[pltpu.V...]
where the time goes in v6:
time: 43.3 us; the launch traced here: 43.1 us
  Pallas kernels  42.5 us (98%)
  between operations  0.65 us (2%)
    pallas_call x1, Pallas kernels, body(): pl.pallas_call(functools.partial(solve_kernel, sizes), out_shape=[pltpu.V...  38.8 us
    pallas_call x1, Pallas kernels, body(): pl.pallas_call(spread_kernel, out_shape=[pltpu.VMEM((WX, 2, ROWS, LANES),...  2.9 us

profile of v6, /device:TPU:1, one launch (start us, length us, event | category | flops | bytes accessed | tf_op | source)
XLA Modules:
  0.0 43.1 jit_solution(1383081171497516148)
XLA Ops:
  0.6 2.9 %spread.1 = (f32[35,2,80,128]{3,2,1,0:T(8,128)S(1)}, f32[128,128]{1,0:T(8,128)S(1)}, f32[128,128]{1,0:T(8,128)S(1)}, f32[128,128]{1,0:T(8,128)S(1)}, f32[8,128]{1,0:T(8,128)S(1)}) custom-call(s32[128]{0:T(128)} %count_hbm.1, s32[3,128]{1,0:T(4,128)} %base_hbm.3, f32[3]{0:T(128)} %reach_hbm.1, f32[12,16384]{1,0:T(8,128)} %w_hbm.3, f32[128,128]{1,0:T(8,128)} %bitcast.9, ...), custom_call_target="tpu_custom_call" | custom-call | tf_op jit(solution)/shard_map/spread/pallas_call | solution.py:830
  3.5 38.8 %solve.1 = (f32[128,128]{1,0:T(8,128)S(1)}, f32[1,128]{1,0:T(1,128)S(1)}, f32[128,128]{1,0:T(8,128)S(1)}) custom-call(s32[3,128]{1,0:T(4,128)} %base_hbm.3, f32[128,128]{1,0:T(8,128)} %bitcast.7, f32[128,128]{1,0:T(8,128)} %bitcast.8, f32[12,16384]{1,0:T(8,128)} %w_hbm.3, f32[8,128]{1,0:T(8,128)S(1)} %get-tuple-element.14.lengths, ...), custom_call_target="tpu_custom_call" | custom-call | tf_op jit(solution)/shard_map/solve/pallas_call | solution.py:856
  42.4 0.8 %update.1 = (f32[128,128]{1,0:T(8,128)}, f32[128,128]{1,0:T(8,128)}, f32[128,128]{1,0:T(8,128)}) custom-call(f32[1,128]{1,0:T(1,128)S(1)} %get-tuple-element.19.sums, f32[128,128]{1,0:T(8,128)S(1)} %get-tuple-element.20.iterate, f32[128,128]{1,0:T(8,128)S(1)} %get-tuple-element.18.live, f32[128,128]{1,0:T(8,128)S(1)} %get-tuple-element.16.live_dir, ...), custom_call_target="tpu_custom_call" | custom-call | tf_op jit(solution)/shard_map/update/pallas_call | solution.py:929

commit v7 on v6

--- a/solution.py
+++ b/solution.py
@@ -519,6 +519,13 @@
             both = jnp.where(copy_of == j, value, both)
         y_msg[side, SIDE : SIDE + 8, :] = beside
         diagonal[side] = both
+    d_copies = {}
+    for ky in range(1, n_gy):
+        for kz in range(1, n_gz):
+            index = (ky - 1) * (n_gz - 1) + kz - 1
+            d_copies[ky, kz] = send(
+                diagonal.at[way(py, ky, n_gy)], diagonal_in.at[index], d_sem, index, at_yz(ky, kz)
+            )
     z_copies += [
         send(z_out.at[way(pz, k, n_gz), late], z_in.at[k - 1, late], z_sem, k + 2, at_yz(0, k))
         for k in range(1, n_gz)
@@ -528,13 +535,6 @@
         for k in range(1, n_gy)
     ]
     send_fixes(rest_fix, 2)
-    d_copies = {}
-    for ky in range(1, n_gy):
-        for kz in range(1, n_gz):
-            index = (ky - 1) * (n_gz - 1) + kz - 1
-            d_copies[ky, kz] = send(
-                diagonal.at[way(py, ky, n_gy)], diagonal_in.at[index], d_sem, index, at_yz(ky, kz)
-            )
 
     copies_in[0].wait()
 
@@ -618,19 +618,6 @@
             jnp.where(channel >= 3, jnp.where(is_moment, right, next_right), 0.0),
         )
 
-    from_z = [[jnp.zeros((8, LANES), F32) for _ in range(PAIRS)] for _ in range(2)]
-    for k in range(1, n_gz):
-        z_copies[k - 1].wait_recv()
-        z_copies[k + n_gz - 2].wait_recv()
-        weights = [jnp.where(is_moment, moment, fix) for moment, fix in mix(pz, n_gz, NZ, length_z, k)]
-        for pair in range(PAIRS):
-            got = z_in[k - 1, pair_place(pair)]
-            for side in range(2):
-                from_z[side][pair] = from_z[side][pair] + weights[side] * got
-    for pair in range(PAIRS):
-        one, two = from_z[0][pair], from_z[1][pair]
-        z_mixed[2 * pair] = jnp.where(first_kinds, one, pltpu.roll(two, 3, 1))
-        z_mixed[2 * pair + 1] = jnp.where(first_kinds, pltpu.roll(one, LANES - 3, 1), two)
     beside = [jnp.zeros((8, LANES), F32) for _ in range(2)]
     both = [jnp.zeros((8, LANES), F32) for _ in range(2)]
     lines = [[jnp.zeros((8, LANES), F32) for _ in range(XROWS // 8)] for _ in range(2)]
@@ -643,12 +630,6 @@
             for tile in range(XROWS // 8):
                 lines[side][tile] = lines[side][tile] + moment * y_in[ky - 1, 8 * tile : 8 * tile + 8, :]
             beside[side] = beside[side] + jnp.where(lane < 40, moment, fix) * y_in[ky - 1, SIDE : SIDE + 8, :]
-        for kz in range(1, n_gz):
-            d_copies[ky, kz].wait_recv()
-            got = channel_weights(kz) * diagonal_in[(ky - 1) * (n_gz - 1) + kz - 1]
-            for side in range(2):
-                moment, fix = weights[side]
-                both[side] = both[side] + jnp.where(copy_of < 5, moment, fix) * got
     for right, left in y_fixes:
         pl.when(py > 0)(right.wait_recv)
         pl.when(py + 1 < n_gy)(left.wait_recv)
@@ -657,15 +638,8 @@
             y_mixed[side, 0, 0, 8 * tile : 8 * tile + 8, :] = lines[side][tile]
         for kind in range(1, 3):
             y_mixed[side, kind, 0] = jnp.where(valid, y_fix_in[side, kind - 1], 0.0)
-        for j in range(15):
-            kind, xt = divmod(j, 5)
-            moved = pltpu.roll(beside[side], LANES - 8 * j, 1) if j else beside[side]
-            y_mixed[side, kind, 1, 8 * xt : 8 * xt + 8, :] = jnp.where(
-                lane < SPARE, moved, jnp.where(copy_of == j, both[side], 0.0)
-            )
-
-    def expand(x, carry):
-        for half in range(2):
+    def expand(half, x, carry):
+        for half in (half,):
             line = [
                 [y_mixed[side, kind, half, pl.ds(line_row(x), 1), :] for kind in range(3)] for side in range(2)
             ]
@@ -687,7 +661,37 @@
                 smooth[x, half, rows, :] = value
         return carry
 
-    lax.fori_loop(0, WX, expand, 0, unroll=5)
+    lax.fori_loop(0, WX, functools.partial(expand, 0), 0, unroll=5)
+    from_z = [[jnp.zeros((8, LANES), F32) for _ in range(PAIRS)] for _ in range(2)]
+    for k in range(1, n_gz):
+        z_copies[k - 1].wait_recv()
+        z_copies[k + n_gz - 2].wait_recv()
+        weights = [jnp.where(is_moment, moment, fix) for moment, fix in mix(pz, n_gz, NZ, length_z, k)]
+        for pair in range(PAIRS):
+            got = z_in[k - 1, pair_place(pair)]
+            for side in range(2):
+                from_z[side][pair] = from_z[side][pair] + weights[side] * got
+    for pair in range(PAIRS):
+        one, two = from_z[0][pair], from_z[1][pair]
+        z_mixed[2 * pair] = jnp.where(first_kinds, one, pltpu.roll(two, 3, 1))
+        z_mixed[2 * pair + 1] = jnp.where(first_kinds, pltpu.roll(one, LANES - 3, 1), two)
+    for ky in range(1, n_gy):
+        weights = mix(py, n_gy, NY, length_y, ky)
+        for kz in range(1, n_gz):
+            d_copies[ky, kz].wait_recv()
+            got = channel_weights(kz) * diagonal_in[(ky - 1) * (n_gz - 1) + kz - 1]
+            for side in range(2):
+                moment, fix = weights[side]
+                both[side] = both[side] + jnp.where(copy_of < 5, moment, fix) * got
+    for side in range(2):
+        for j in range(15):
+            kind, xt = divmod(j, 5)
+            moved = pltpu.roll(beside[side], LANES - 8 * j, 1) if j else beside[side]
+            y_mixed[side, kind, 1, 8 * xt : 8 * xt + 8, :] = jnp.where(
+                lane < SPARE, moved, jnp.where(copy_of == j, both[side], 0.0)
+            )
+
+    lax.fori_loop(0, WX, functools.partial(expand, 1), 0, unroll=5)
 
     def tile_spot(t):
         at = pl.ds(pl.multiple_of(t * LANES, LANES), LANES)

time: 43.3 us -> 43.2 us (level)
  no operation moved by 1% of the time
where the time goes in v7:
time: 43.2 us; the launch traced here: 43.1 us
  Pallas kernels  42.5 us (98%)
  between operations  0.65 us (2%)
    pallas_call x1, Pallas kernels, body(): pl.pallas_call(functools.partial(solve_kernel, sizes), out_shape=[pltpu.V...  38.8 us
    pallas_call x1, Pallas kernels, body(): pl.pallas_call(spread_kernel, out_shape=[pltpu.VMEM((WX, 2, ROWS, LANES),...  2.89 us

profile of v7, /device:TPU:1, one launch (start us, length us, event | category | flops | bytes accessed | tf_op | source)
XLA Modules:
  0.0 43.1 jit_solution(2578872826224827734)
XLA Ops:
  0.6 2.9 %spread.1 = (f32[35,2,80,128]{3,2,1,0:T(8,128)S(1)}, f32[128,128]{1,0:T(8,128)S(1)}, f32[128,128]{1,0:T(8,128)S(1)}, f32[128,128]{1,0:T(8,128)S(1)}, f32[8,128]{1,0:T(8,128)S(1)}) custom-call(s32[128]{0:T(128)} %count_hbm.1, s32[3,128]{1,0:T(4,128)} %base_hbm.3, f32[3]{0:T(128)} %reach_hbm.1, f32[12,16384]{1,0:T(8,128)} %w_hbm.3, f32[128,128]{1,0:T(8,128)} %bitcast.9, ...), custom_call_target="tpu_custom_call" | custom-call | tf_op jit(solution)/shard_map/spread/pallas_call | solution.py:834
  3.5 38.8 %solve.1 = (f32[128,128]{1,0:T(8,128)S(1)}, f32[1,128]{1,0:T(1,128)S(1)}, f32[128,128]{1,0:T(8,128)S(1)}) custom-call(s32[3,128]{1,0:T(4,128)} %base_hbm.3, f32[128,128]{1,0:T(8,128)} %bitcast.7, f32[128,128]{1,0:T(8,128)} %bitcast.8, f32[12,16384]{1,0:T(8,128)} %w_hbm.3, f32[8,128]{1,0:T(8,128)S(1)} %get-tuple-element.14.lengths, ...), custom_call_target="tpu_custom_call" | custom-call | tf_op jit(solution)/shard_map/solve/pallas_call | solution.py:860
  42.4 0.8 %update.1 = (f32[128,128]{1,0:T(8,128)}, f32[128,128]{1,0:T(8,128)}, f32[128,128]{1,0:T(8,128)}) custom-call(f32[1,128]{1,0:T(1,128)S(1)} %get-tuple-element.19.sums, f32[128,128]{1,0:T(8,128)S(1)} %get-tuple-element.20.iterate, f32[128,128]{1,0:T(8,128)S(1)} %get-tuple-element.18.live, f32[128,128]{1,0:T(8,128)S(1)} %get-tuple-element.16.live_dir, ...), custom_call_target="tpu_custom_call" | custom-call | tf_op jit(solution)/shard_map/update/pallas_call | solution.py:933
